TPU v7x, 512 devices: a whole 4x4x16 slice. The times are simulated.
512 devices in a mesh: elem: 128 (over z, y, x_hi), mp: 4 (over x_lo, core).
Axes of the slice: x: 4 (x_hi: 2, x_lo: 2; x = x_hi * 2 + x_lo), y: 4, z: 16, core: 2. Of those that a mesh axis runs over, the one named last changes fastest.
Arguments:
- state_field: float32 [49, 1536, 128], P(None, 'elem'), may hold values from -6 to 6
- diffusion: float32 [128], replicated, may hold values from 0.01 to 0.05
- stretch_of_column: int32 [32, 1024], P(None, 'elem'), may hold values from -1 to 127, as said below
- w_in: bfloat16 [16, 512], replicated, may hold values from -1.5 to 1.5
- level_embed: bfloat16 [8, 512], replicated, may hold values from -6 to 6
- w_qkv: bfloat16 [3, 512, 512], P(None, None, 'mp'), may hold values from -0.25 to 0.25
- w_out: bfloat16 [512, 512], P('mp'), may hold values from -0.25 to 0.25
- w_up: bfloat16 [512, 2048], P(None, 'mp'), may hold values from -0.25 to 0.25
- w_down: bfloat16 [2048, 512], P('mp'), may hold values from -0.125 to 0.125
- w_read: float32 [512, 16], replicated, may hold values from -0.25 to 0.25
Outputs:
- new_state: float32 [49, 1536, 128], P(None, 'elem')
- tendency: float32 [32, 1024, 128], P(None, 'elem')
Inputs may be any that keep to these rules, and one draw needn't show every extreme that they name: `stretch_of_column`: exactly 128 columns of the whole array name each stretch (batch); a column's results don't depend on which batch it is in. Within the columns of one index of elem no stretch is named more than 2 times, and some stretch exactly 2 times. How many columns of one index of elem name a stretch varies from 0 to 256 over the indices.
All inputs are finite; a program needn't handle non-finite values.
Results may differ from a plain program's by a relative error of at most 0.0042.
Values may be sent and summed in bfloat16 or wider, within the bound.
A program may use at most 64 MiB of HBM per device.

v0:
```python
import math

import jax
import jax.numpy as jnp
import numpy as np
from jax import lax
from jax.sharding import PartitionSpec as P

HEADS = 8


def shifted(x, axis, by):
    devices = lax.axis_size(axis)
    return lax.ppermute(x, axis, [(i, (i + by) % devices) for i in range(devices)])


def basis_weight(points, index):
    return np.prod([points[index] - points[other] for other in range(4) if other != index])


def gll_tables():
    points = np.array([-1.0, -1.0 / math.sqrt(5.0), 1.0 / math.sqrt(5.0), 1.0])
    quadrature = np.array([1.0, 5.0, 5.0, 1.0]) / 6.0
    derivative = np.zeros((4, 4))
    for row_index in range(4):
        for col_index in range(4):
            if row_index == col_index:
                derivative[row_index, col_index] = sum(
                    (
                        1.0 / (points[row_index] - points[other])
                        for other in range(4)
                        if other != row_index
                    )
                )
            else:
                derivative[row_index, col_index] = (
                    basis_weight(points, row_index)
                    / basis_weight(points, col_index)
                    / (points[row_index] - points[col_index])
                )
    remap = np.array([[0.375, 0.5, 0.125, 0.0], [0.0, 0.125, 0.5, 0.375]])
    return (derivative.astype(np.float32), quadrature.astype(np.float32), remap.astype(np.float32))


def elements(extended, cells_y, cells_x):
    node_rows = extended.shape[0]
    feature = extended.shape[2]
    inner_x = extended[:, : 3 * cells_x].reshape(node_rows, cells_x, 3, feature)
    edge_x = extended[:, 3 : 3 * cells_x + 1 : 3][:, :, None]
    along_x = jnp.concatenate([inner_x, edge_x], axis=2)
    inner_y = along_x[: 3 * cells_y].reshape(cells_y, 3, cells_x, 4, feature)
    edge_y = along_x[3 : 3 * cells_y + 1 : 3][:, None]
    return jnp.concatenate([inner_y, edge_y], axis=1)


def stiffness(nodal, derivative, quadrature):
    dmat = jnp.asarray(derivative)
    weight = jnp.asarray(quadrature)
    grad_x = jnp.einsum("ik,ybxkf->ybxif", dmat, nodal, precision=lax.Precision.HIGHEST)
    grad_y = jnp.einsum("jk,ykxaf->yjxaf", dmat, nodal, precision=lax.Precision.HIGHEST)
    weighted = dmat * weight[:, None]
    term_x = jnp.einsum("ia,ybxif->ybxaf", weighted, grad_x, precision=lax.Precision.HIGHEST)
    term_y = jnp.einsum("jb,yjxaf->ybxaf", weighted, grad_y, precision=lax.Precision.HIGHEST)
    return -(
        weight[None, :, None, None, None] * term_x + weight[None, None, None, :, None] * term_y
    )


def assemble_rows(stiff):
    cells_y, _, cells_x, _, feature = stiff.shape
    inner = stiff[:, :3].reshape(3 * cells_y, cells_x, 4, feature)
    inner = jnp.pad(inner, ((0, 1), (0, 0), (0, 0), (0, 0)))
    zero_part = jnp.zeros_like(stiff[:, 3])
    trailing = jnp.stack([zero_part, zero_part, stiff[:, 3]], axis=1).reshape(
        3 * cells_y, cells_x, 4, feature
    )
    trailing = jnp.pad(trailing, ((1, 0), (0, 0), (0, 0), (0, 0)))
    return inner + trailing


def node_mass(node_rows, node_cols):
    row_index = jnp.arange(node_rows)
    col_index = jnp.arange(node_cols)
    mass_y = jnp.where(
        (row_index == 0) | (row_index == node_rows - 1),
        1.0 / 6.0,
        jnp.where(row_index % 3 == 0, 1.0 / 3.0, 5.0 / 6.0),
    )
    mass_x = jnp.where(col_index % 3 == 0, 1.0 / 3.0, 5.0 / 6.0)
    return (mass_y[:, None] * mass_x[None, :]).astype(jnp.float32)


def with_east(field):
    eastern = shifted(field[:, :1], "elem", -1)
    return jnp.concatenate([field, eastern], axis=1)


def physics(columns, w_in, level_embed, w_qkv, w_out, w_up, w_down, w_read):
    count = columns.shape[0]
    nvar = w_in.shape[0]
    width = w_in.shape[1]
    levels = level_embed.shape[0]
    head_dim = width // HEADS
    per_level = columns.reshape(count * levels, nvar)
    embed = jnp.dot(per_level, w_in, preferred_element_type=jnp.float32).reshape(
        count, levels, width
    )
    embed = (embed + level_embed.astype(jnp.float32)[None]).reshape(count * levels, width)
    normed = (embed * lax.rsqrt(jnp.mean(embed * embed, axis=-1, keepdims=True) + 1e-05)).astype(
        jnp.bfloat16
    )
    query = jnp.dot(normed, w_qkv[0], preferred_element_type=jnp.float32).astype(jnp.bfloat16)
    keys = jnp.dot(normed, w_qkv[1], preferred_element_type=jnp.float32).astype(jnp.bfloat16)
    values = jnp.dot(normed, w_qkv[2], preferred_element_type=jnp.float32).astype(jnp.bfloat16)
    local_heads = w_qkv.shape[2] // head_dim
    query = query.reshape(count, levels, local_heads, head_dim)
    keys = keys.reshape(count, levels, local_heads, head_dim)
    values = values.reshape(count, levels, local_heads, head_dim)
    scores = jnp.einsum("nlhd,nmhd->nhlm", query, keys, preferred_element_type=jnp.float32) * (
        1.0 / math.sqrt(head_dim)
    )
    expo = jnp.exp(scores)
    prob = (expo / jnp.sum(expo, axis=-1, keepdims=True)).astype(jnp.bfloat16)
    mixed = jnp.einsum("nhlm,nmhd->nlhd", prob, values, preferred_element_type=jnp.float32).astype(
        jnp.bfloat16
    )
    mixed = mixed.reshape(count * levels, local_heads * head_dim)
    attended = jnp.dot(mixed, w_out, preferred_element_type=jnp.float32)
    hidden = jax.nn.gelu(
        jnp.dot(normed, w_up, preferred_element_type=jnp.float32), approximate=True
    ).astype(jnp.bfloat16)
    processed = jnp.dot(hidden, w_down, preferred_element_type=jnp.float32)
    partial_read = jnp.dot(attended + processed, w_read, precision=lax.Precision.HIGHEST).reshape(
        count, levels * nvar
    )
    summed = lax.psum(partial_read, "mp")
    own_read = jnp.dot(embed, w_read, precision=lax.Precision.HIGHEST).reshape(count, levels * nvar)
    return summed + own_read


def local(
    state_field, diffusion, stretch_of_column, w_in, level_embed, w_qkv, w_out, w_up, w_down, w_read
):
    derivative, quadrature, remap = gll_tables()
    node_rows = state_field.shape[0]
    node_cols = state_field.shape[1]
    feature = state_field.shape[2]
    cells_y = (node_rows - 1) // 3
    cells_x = node_cols // 3
    stiff = stiffness(elements(with_east(state_field), cells_y, cells_x), derivative, quadrature)
    gathered = assemble_rows(stiff)
    inner_cols = gathered[:, :, :3].reshape(node_rows, node_cols, feature)
    zero_part = jnp.zeros_like(gathered[:, :, 3])
    trailing = jnp.stack([zero_part, zero_part, gathered[:, :, 3]], axis=2).reshape(
        node_rows, node_cols, feature
    )
    incoming = shifted(trailing[:, -1:], "elem", 1)
    assembled = inner_cols + jnp.concatenate([incoming, trailing[:, :-1]], axis=1)
    new_state = state_field + diffusion * (assembled / node_mass(node_rows, node_cols)[:, :, None])
    fine = elements(with_east(new_state), cells_y, cells_x)
    remap_table = jnp.asarray(remap)
    columns = jnp.einsum(
        "cb,da,ybxaf->ycxdf", remap_table, remap_table, fine, precision=lax.Precision.HIGHEST
    )
    columns = columns.reshape(4 * cells_y * cells_x, feature).astype(jnp.bfloat16)
    stretch_flat = stretch_of_column.reshape(-1)
    live = stretch_flat >= 0
    results = physics(columns, w_in, level_embed, w_qkv, w_out, w_up, w_down, w_read)
    tend_flat = jnp.where(live[:, None], results, 0.0)
    tendency = tend_flat.reshape(2 * cells_y, 2 * cells_x, feature)
    return (new_state, tendency)


def solution(mesh):
    in_specs = (
        P(None, "elem", None),
        P(),
        P(None, "elem"),
        P(),
        P(),
        P(None, None, "mp"),
        P("mp", None),
        P(None, "mp"),
        P("mp", None),
        P(),
    )
    out_specs = (P(None, "elem", None), P(None, "elem", None))
    return jax.shard_map(local, mesh=mesh, in_specs=in_specs, out_specs=out_specs, check_vma=False)
```

profile of v0, /device:TPU:1, one launch (start us, length us, event | category | flops | bytes accessed | tf_op | source)
XLA Modules:
  0.0 152.7 jit_solution(17089194987867273846)
XLA Ops:
  7.2 0.8 slice.51
  8.1 16.9 %collective-permute-start = (f32[49,1,128]{2,1,0:T(1,128)S(1)}, f32[49,1,128]{2,1,0:T(1,128)S(1)}, u32[]{:S(2)}, u32[]{:S(2)}) collective-permute-start(f32[49,1,128]{2,1,0:T(1,128)S(1)} %copy.132), channel_id=1, source_target_pairs={{0,508},{4,0},{8,4},{12,8},{16,12},{20,16},{24,20},{28,24},{32,28}... | collective-permute-start | bytes 75272 | tf_op jit(solution)/shard_map/ppermute | solution.py:14
  25.1 1.0 copy.145
  26.1 1.1 copy.134
  27.3 0.6 slice.52
  27.9 0.2 fusion.45
  28.0 0.2 pad_maximum_fusion.1
  28.4 1.0 convolution_bitcast_fusion.1
  29.5 1.1 convolution_bitcast_fusion
  30.6 1.0 fusion.61
  31.6 1.0 fusion.60
  32.6 0.6 fusion.38
  33.3 0.2 copy.138
  33.6 0.2 pad_add_fusion
  33.9 1.9 %collective-permute-start.1 = (f32[49,1,128]{2,1,0:T(1,128)S(1)}, f32[49,1,128]{2,1,0:T(1,128)S(1)}, u32[]{:S(2)}, u32[]{:S(2)}) collective-permute-start(f32[49,1,128]{2,1,0:T(1,128)S(1)} %copy.170), channel_id=1, source_target_pairs={{0,4},{4,8},{8,12},{12,16},{16,20},{20,24},{24,28},{28,32},{32,36}... | collective-permute-start | bytes 75272 | tf_op jit(solution)/shard_map/ppermute | solution.py:14
  36.2 8.0 %collective-permute-done.1 = f32[49,1,128]{2,1,0:T(1,128)S(1)} collective-permute-done((f32[49,1,128]{2,1,0:T(1,128)S(1)}, f32[49,1,128]{2,1,0:T(1,128)S(1)}, u32[]{:S(2)}, u32[]{:S(2)}) %collective-permute-start.1) | collective-permute-done | bytes 25120 | tf_op jit(solution)/shard_map/ppermute | solution.py:14
  44.2 0.2 fusion.43
  44.5 3.8 %collective-permute-start.2 = (f32[49,1,128]{2,1,0:T(1,128)S(1)}, f32[49,1,128]{2,1,0:T(1,128)S(1)}, u32[]{:S(2)}, u32[]{:S(2)}) collective-permute-start(f32[49,1,128]{2,1,0:T(1,128)S(1)} %slice.76), channel_id=1, source_target_pairs={{0,508},{4,0},{8,4},{12,8},{16,12},{20,16},{24,20},{28,24},{32,28}... | collective-permute-start | bytes 75272 | tf_op jit(solution)/shard_map/ppermute | solution.py:14
  48.7 1.8 %collective-permute-done.2 = f32[49,1,128]{2,1,0:T(1,128)S(1)} collective-permute-done((f32[49,1,128]{2,1,0:T(1,128)S(1)}, f32[49,1,128]{2,1,0:T(1,128)S(1)}, u32[]{:S(2)}, u32[]{:S(2)}) %collective-permute-start.2) | collective-permute-done | bytes 25120 | tf_op jit(solution)/shard_map/ppermute | solution.py:14
  50.6 0.8 slice.62
  51.4 0.2 fusion.44
  51.6 0.2 pad_maximum_fusion.2
  51.8 0.2 copy.149
  52.0 1.2 fusion.34
  53.2 0.6 fusion.29
  53.8 0.4 convert_element_type.51
  54.2 2.6 %multiply_reduce_fusion = (f32[256,8]{0,1:T(8,128)S(1)}, f32[256,8,512]{2,0,1:T(8,128)}) fusion(f32[8,512]{1,0:T(8,128)S(1)} %convert_element_type.52, bf16[16,512]{1,0:T(8,128)(2,1)S(1)} %copy-done.5, bf16[256,8,16]{2,1,0:T(8,128)(2,1)S(1)} %convert_element_type.51), kind=kOutput, calls=%fused_computation.16 | convolution fusion | flops 36698112 | bytes 4300800 | tf_op jit(solution)/shard_map/dot_general | solution.py:105
  57.0 2.5 %multiply_convert_fusion = bf16[256,8,512]{2,0,1:T(8,128)(2,1)S(1)} fusion(f32[256,8,512]{2,0,1:T(8,128)} %get-tuple-element.13, f32[256,8]{0,1:T(8,128)S(1)} %add_rsqrt_fusion), kind=kLoop, calls=%fused_computation.15 | loop fusion | flops 2097152 | bytes 6299648 | tf_op jit(solution)/shard_map/convert_element_type | solution.py:109
  59.5 1.3 convolution_convert_fusion
  60.9 1.3 convolution_convert_fusion.1
  62.2 1.3 convolution_convert_fusion.2
  63.7 1.4 reshape.173
  65.1 1.4 reshape.171
  66.5 1.4 reshape.172
  67.9 2.2 %fusion.31 = f32[256,2,8,8]{2,3,1,0:T(8,128)S(1)} fusion(bf16[256,8,2,64]{3,2,1,0:T(2,128)(2,1)} %reshape.173, bf16[256,8,2,64]{3,2,1,0:T(2,128)(2,1)} %reshape.172), kind=kOutput, calls=%fused_computation.38 | convolution fusion | flops 4194304 | bytes 1179648 | tf_op jit(solution)/shard_map/nlhd,nmhd->nhlm/dot_general | solution.py:119
  70.1 1.0 copy.156
  71.3 0.9 copy.158
  72.2 2.1 %fusion.28 = bf16[256,8,2,64]{3,1,2,0:T(8,128)(2,1)S(1)} fusion(bf16[256,2,8,8]{3,2,1,0:T(8,128)(2,1)S(1)} %copy.158, bf16[256,8,2,64]{3,2,1,0:T(2,128)(2,1)} %reshape.171), kind=kOutput, calls=%fused_computation.32 | convolution fusion | flops 4456448 | bytes 1114112 | tf_op jit(solution)/shard_map/nhlm,nmhd->nlhd/dot_general | solution.py:124
  74.4 1.1 copy.159
  75.5 0.5 reshape.174
  76.0 2.7 %fusion.62 = f32[2048,512]{1,0:T(8,128)} fusion(bf16[2048,128]{1,0:T(8,128)(2,1)S(1)} %reshape.174, bf16[128,512]{1,0:T(8,128)(2,1)S(1)} %copy-done.4), kind=kOutput, calls=%fused_computation.95 | convolution fusion | flops 268435456 | bytes 4849664 | tf_op jit(solution)/shard_map/dot_general | solution.py:128
  78.6 8.6 %fusion.26 = f32[2048,512]{1,0:T(8,128)} fusion(bf16[512,512]{1,0:T(8,128)(2,1)S(1)} %copy-done, bf16[512,512]{1,0:T(8,128)(2,1)S(1)} %copy-done.13, f32[256,8,512]{2,0,1:T(8,128)} %get-tuple-element.13, f32[2048]{0:T(1024)S(1)} %rsqrt.13), kind=kOutput, calls=%fused_computation.30 | convolution fusion | flops 2159017984 | bytes 9445376 | tf_op jit(solution)/shard_map/dot_general | solution.py:132
  87.2 5.8 %fusion.11 = f32[2048,16]{1,0:T(8,128)S(1)} fusion(f32[512,16]{0,1:T(8,128)S(1)} %copy-done.3, f32[2048,512]{1,0:T(8,128)} %fusion.62, f32[2048,512]{1,0:T(8,128)} %fusion.26), kind=kOutput, calls=%fused_computation.13 | convolution fusion | flops 202375168 | bytes 8552448 | tf_op jit(solution)/shard_map/dot_general | solution.py:133
  93.0 1.0 reshape.176
  94.0 7.6 %fusion.8 = f32[2048,16]{1,0:T(8,128)S(1)} fusion(f32[512,16]{0,1:T(8,128)S(1)} %copy-done.3, f32[256,8,512]{2,0,1:T(8,128)} %get-tuple-element.13), kind=kOutput, calls=%fused_computation.9 | convolution fusion | flops 201326592 | bytes 4358144 | tf_op jit(solution)/shard_map/dot_general | solution.py:137
  101.6 0.3 reshape.177
  101.9 42.3 %all-reduce.6.cloned.1.call-done = f32[256,128]{1,0:T(8,128)} async-done(((f32[256,128]{1,0:T(8,128)}), f32[256,128]{1,0:T(8,128)}) %all-reduce.6.cloned.1.call-update) | async-done | bytes 131088 | tf_op jit(solution)/shard_map/psum | solution.py:136
  144.2 1.7 %select_bitcast_fusion = f32[32,8,128]{2,1,0:T(8,128)} fusion(f32[256,128]{1,0:T(8,128)} %all-reduce.6.cloned.1.call-done, f32[256,128]{1,0:T(8,128)S(1)} %reshape.177, pred[256]{0:T(512)(128)(4,1)S(1)} %ge.15), kind=kLoop, calls=%fused_computation.69 | loop fusion | flops 65536 | bytes 393472 | tf_op jit(solution)/shard_map/reshape | solution.py:170
  (67 shorter events, 1.8 us)
Async XLA Ops:
  7.2 71.5 %copy-start = (bf16[512,512]{1,0:T(8,128)(2,1)S(1)}, bf16[512,512]{1,0:T(8,128)(2,1)}, u32[]{:S(2)}) copy-start(bf16[512,512]{1,0:T(8,128)(2,1)} %param.21) | copy-start | bytes 1572868
  7.2 21.2 %copy-start.6 = (f32[4,4,1,1,1]{1,0,4,3,2:T(4,128)S(1)}, f32[4,4,1,1,1]{1,0,4,3,2:T(4,128)}, u32[]{:S(2)}) copy-start(f32[4,4,1,1,1]{1,0,4,3,2:T(4,128)} %constant.70) | copy-start | bytes 196
  7.2 23.4 %copy-start.7 = (f32[4,4,1,1,1]{0,1,4,3,2:T(4,128)S(1)}, f32[4,4,1,1,1]{0,1,4,3,2:T(4,128)}, u32[]{:S(2)}) copy-start(f32[4,4,1,1,1]{0,1,4,3,2:T(4,128)} %constant.71) | copy-start | bytes 196
  7.2 137.0 %all-reduce.6.cloned.1.call-start = ((), (), s32[]{:S(2)}) async-start(), calls=%async_computation | async-start | bytes 262144 | tf_op jit(solution)/shard_map/psum | solution.py:136
  8.1 19.1 %collective-permute-start = (f32[49,1,128]{2,1,0:T(1,128)S(1)}, f32[49,1,128]{2,1,0:T(1,128)S(1)}, u32[]{:S(2)}, u32[]{:S(2)}) collective-permute-start(f32[49,1,128]{2,1,0:T(1,128)S(1)} %copy.132), channel_id=1, source_target_pairs={{0,508},{4,0},{8,4},{12,8},{16,12},{20,16},{24,20},{28,24},{32,28}... | collective-permute-start | bytes 75272 | tf_op jit(solution)/shard_map/ppermute | solution.py:14
  27.2 5.4 %copy-start.11 = (f32[4]{0:T(128)S(1)}, f32[4]{0:T(128)}, u32[]{:S(2)}) copy-start(f32[4]{0:T(128)} %constant.57.clone) | copy-start | bytes 52
  32.6 11.6 %copy-start.1 = (f32[49,12,128]{2,0,1:T(8,128)S(1)}, f32[49,12,128]{2,0,1:T(8,128)}, u32[]{:S(2)}) copy-start(f32[49,12,128]{2,0,1:T(8,128)} %param.13) | copy-start | bytes 903172
  32.6 11.6 %copy-start.12 = (f32[128]{0:T(128)S(1)}, f32[128]{0:T(128)}, u32[]{:S(2)}) copy-start(f32[128]{0:T(128)} %param.14) | copy-start | bytes 1540
  33.3 15.0 %copy-start.9 = (s32[32,8]{0,1:T(8,128)S(1)}, s32[32,8]{0,1:T(8,128)}, u32[]{:S(2)}) copy-start(s32[32,8]{0,1:T(8,128)} %param.15) | copy-start | bytes 3076
  33.3 15.2 %copy-start.8 = (bf16[8,512]{1,0:T(8,128)(2,1)S(1)}, bf16[8,512]{1,0:T(8,128)(2,1)}, u32[]{:S(2)}) copy-start(bf16[8,512]{1,0:T(8,128)(2,1)} %param.17) | copy-start | bytes 24580
  33.9 10.3 %collective-permute-start.1 = (f32[49,1,128]{2,1,0:T(1,128)S(1)}, f32[49,1,128]{2,1,0:T(1,128)S(1)}, u32[]{:S(2)}, u32[]{:S(2)}) collective-permute-start(f32[49,1,128]{2,1,0:T(1,128)S(1)} %copy.170), channel_id=1, source_target_pairs={{0,4},{4,8},{8,12},{12,16},{16,20},{20,24},{24,28},{28,32},{32,36}... | collective-permute-start | bytes 75272 | tf_op jit(solution)/shard_map/ppermute | solution.py:14
  36.0 16.0 %copy-start.10 = (f32[2,4,1,1,1]{1,0,4,3,2:T(2,128)S(1)}, f32[2,4,1,1,1]{1,0,4,3,2:T(2,128)}, u32[]{:S(2)}) copy-start(f32[2,4,1,1,1]{1,0,4,3,2:T(2,128)} %constant.72) | copy-start | bytes 100
  44.2 10.0 %copy-start.5 = (bf16[16,512]{1,0:T(8,128)(2,1)S(1)}, bf16[16,512]{1,0:T(8,128)(2,1)}, u32[]{:S(2)}) copy-start(bf16[16,512]{1,0:T(8,128)(2,1)} %param.16) | copy-start | bytes 49156
  44.5 6.1 %collective-permute-start.2 = (f32[49,1,128]{2,1,0:T(1,128)S(1)}, f32[49,1,128]{2,1,0:T(1,128)S(1)}, u32[]{:S(2)}, u32[]{:S(2)}) collective-permute-start(f32[49,1,128]{2,1,0:T(1,128)S(1)} %slice.76), channel_id=1, source_target_pairs={{0,508},{4,0},{8,4},{12,8},{16,12},{20,16},{24,20},{28,24},{32,28}... | collective-permute-start | bytes 75272 | tf_op jit(solution)/shard_map/ppermute | solution.py:14
  48.6 8.2 %copy-start.2 = (f32[49,12,128]{2,0,1:T(8,128)}, f32[49,12,128]{2,0,1:T(8,128)S(1)}, u32[]{:S(2)}) copy-start(f32[49,12,128]{2,0,1:T(8,128)S(1)} %copy.164) | copy-start | bytes 903172
  56.8 2.7 %copy-start.14 = (bf16[3,512,128]{2,1,0:T(8,128)(2,1)S(1)}, bf16[3,512,128]{2,1,0:T(8,128)(2,1)}, u32[]{:S(2)}) copy-start(bf16[3,512,128]{2,1,0:T(8,128)(2,1)} %param.18) | copy-start | bytes 1179652
  71.2 4.8 %copy-start.4 = (bf16[128,512]{1,0:T(8,128)(2,1)S(1)}, bf16[128,512]{1,0:T(8,128)(2,1)}, u32[]{:S(2)}) copy-start(bf16[128,512]{1,0:T(8,128)(2,1)} %param.19) | copy-start | bytes 393220
  74.4 4.3 %copy-start.13 = (bf16[512,512]{1,0:T(8,128)(2,1)S(1)}, bf16[512,512]{1,0:T(8,128)(2,1)}, u32[]{:S(2)}) copy-start(bf16[512,512]{1,0:T(8,128)(2,1)} %param.20) | copy-start | bytes 1572868
  78.6 8.6 %copy-start.3 = (f32[512,16]{0,1:T(8,128)S(1)}, f32[512,16]{0,1:T(8,128)}, u32[]{:S(2)}) copy-start(f32[512,16]{0,1:T(8,128)} %param.22) | copy-start | bytes 98308
Sparse Core Ops, SparseCore 0:
  94.2 49.9 all-reduce.5
where the time goes:
time: 153 us
  waiting for transfers between devices  52.1 us (34%)
  matrix products  41.5 us (27%)
  starting transfers between devices  22.6 us (15%)
  local copies, waits for them, and re-layouts  15.2 us (10%)
  between operations  14.7 us (10%)
  other arithmetic  6.5 us (4%)
    psum x1, waiting for transfers between devices, physics(): summed = lax.psum(partial_read, 'mp')  42.3 us
    ppermute x3, starting transfers between devices, shifted(): lax.ppermute(x, axis, [(i, (i + by) % devices) for i in range(devices)])  22.6 us
    ppermute x3, waiting for transfers between devices, shifted(): lax.ppermute(x, axis, [(i, (i + by) % devices) for i in range(devices)])  9.84 us
    dot_general x1, matrix products, physics(): processed = jnp.dot(hidden, w_down, preferred_element_type=jnp.float32)  8.6 us
    dot_general x1, matrix products, physics(): jnp.dot(embed, w_read, precision=lax.Precision.HIGHEST)  7.56 us
    dot_general x1, matrix products, physics(): jnp.dot(attended + processed, w_read, precision=lax.Precision.HIGHEST)  5.8 us
  transfers between devices with their start and end apart: 4, of which 3 were waited for; matrix products, arithmetic and copies ran while one was open for 7% of the time, Pallas kernels for 0%

commit v1 on v0

v1 whole, which is shorter than its diff:
```python
import math

import jax
import jax.numpy as jnp
import numpy as np
from jax import lax
from jax.experimental import pallas as pl
from jax.experimental.pallas import tpu as pltpu
from jax.sharding import PartitionSpec as P

MESH = pl.DeviceIdType.MESH
F32 = jnp.float32
BF16 = jnp.bfloat16
HIGHEST = lax.Precision.HIGHEST

LEV = 8
NV = 16
F = 128
HEAD = 64
Y = 49
ROWS = 56
PAD = 8
CELLS = 64
TOK = LEV * CELLS
KU = 32


def stiffness_1d():
    points = np.array([-1.0, -1.0 / math.sqrt(5.0), 1.0 / math.sqrt(5.0), 1.0])
    weight = np.array([1.0, 5.0, 5.0, 1.0]) / 6.0
    basis = [np.prod([points[i] - points[o] for o in range(4) if o != i]) for i in range(4)]
    dmat = np.zeros((4, 4))
    for i in range(4):
        for k in range(4):
            if i == k:
                dmat[i, k] = sum(1.0 / (points[i] - points[o]) for o in range(4) if o != i)
            else:
                dmat[i, k] = basis[i] / basis[k] / (points[i] - points[k])
    return dmat.T @ (weight[:, None] * dmat)


KM = stiffness_1d()


def nt(a, b, precision=None):
    return lax.dot_general(a, b, (((1,), (1,)), ((), ())), precision=precision, preferred_element_type=F32)


def tn(a, b):
    return lax.dot_general(a, b, (((0,), (0,)), ((), ())), preferred_element_type=F32)


def nn(a, b):
    return jnp.dot(a, b, preferred_element_type=F32)


def iota(shape, dim):
    return lax.broadcasted_iota(jnp.int32, shape, dim)


def split2(x):
    high = x.astype(BF16)
    return high, (x - high.astype(F32)).astype(BF16)


def lane_turn(x, by):
    return x if by == 0 else jnp.concatenate([x[:, by:], x[:, :by]], axis=1)


def band_along_y(offset):
    y = iota((ROWS, F), 0)
    kind = y - 3 * ((y * 171) >> 9)
    out = jnp.zeros((ROWS, F), F32)
    if 0 <= offset + 1 < 4:
        out = jnp.where(kind == 1, F32(1.2 * KM[1, offset + 1]), out)
    if 0 <= offset + 2 < 4:
        out = jnp.where(kind == 2, F32(1.2 * KM[2, offset + 2]), out)
    corner = jnp.zeros((ROWS, F), F32)
    if offset >= 0:
        corner = corner + jnp.where(y < Y - 1, F32(KM[0, offset]), F32(0))
    if offset <= 0:
        corner = corner + jnp.where(y > 0, F32(KM[3, offset + 3]), F32(0))
    corner = corner * jnp.where((y == 0) | (y == Y - 1), F32(6), F32(3))
    out = jnp.where(kind == 0, corner, out)
    return jnp.where(y < Y, out, F32(0))


def kernel(
    elems, state, diff, stretch, w_in, lemb, w_qkv, w_out, w_up, w_down, w_read,
    new_out, tend_out,
    st, ext, cy, fresh, n12, f12, gsend, grecv, psend, precv,
    vdiff, vstretch, vin, vlev, vqkv, vwout, vup, vdown, vread,
    msg, natural, tbuf, tend,
    load_sem, out_sem, halo_send, halo_recv, msg_send, msg_recv, t_send, t_recv,
):
    me = lax.axis_index("elem")
    j = lax.axis_index("mp")
    east = lax.rem(me + 1, elems)
    west = lax.rem(me + elems - 1, elems)
    peers = (None, j + 1 - 2 * lax.rem(j, 2), lax.rem(j + 2, 4), 3 - j)

    loads = [
        pltpu.make_async_copy(src, dst, load_sem.at[i])
        for i, (src, dst) in enumerate(
            [
                (state, st), (diff, vdiff), (w_in, vin), (lemb, vlev), (w_read, vread),
                (w_qkv, vqkv), (w_up, vup), (w_out, vwout), (w_down, vdown), (stretch, vstretch),
            ]
        )
    ]
    for copy in loads:
        copy.start()

    barrier = pltpu.get_barrier_semaphore()
    for place in ({"elem": east}, {"elem": west}, {"mp": peers[1]}, {"mp": peers[2]}, {"mp": peers[3]}):
        pl.semaphore_signal(barrier, inc=1, device_id=place, device_id_type=MESH)

    for offset in range(-3, 4):
        cy[offset + 3] = band_along_y(offset)
    ext[:, :, 0:PAD, :] = jnp.zeros((4, 3, PAD, F), F32)
    ext[:, :, PAD + 48 : PAD + 64, :] = jnp.zeros((4, 3, 16, F), F32)

    def far(src, dst, k, place):
        return pltpu.make_async_remote_copy(
            src_ref=src, dst_ref=dst, send_sem=halo_send.at[k], recv_sem=halo_recv.at[k],
            device_id=place, device_id_type=MESH,
        )

    first_row = pl.multiple_of(8 * ((3 * j) // 2), 8)
    send_f = far(state.at[0, 0], f12, 0, {"elem": west})
    send_p = far(psend.at[pl.ds(first_row, 24)], precv, 1, {"elem": west})
    send_g = far(gsend, grecv, 2, {"elem": east})

    pl.semaphore_wait(barrier, 5)
    send_f.start()

    loads[0].wait()
    loads[1].wait()
    ext[:, :, PAD : PAD + Y, :] = st[...]
    d = vdiff[...]
    body = slice(PAD, PAD + ROWS)
    f0, f1, f2, f3 = ext[0, 0, body], ext[0, 1, body], ext[0, 2, body], ext[1, 0, body]
    lap = 3.0 * (F32(2 * KM[0, 0]) * f0 + F32(KM[0, 1]) * f1 + F32(KM[0, 2]) * f2 + F32(KM[0, 3]) * f3)
    for offset in range(-3, 4):
        lap = lap + cy[offset + 3] * ext[0, 0, PAD + offset : PAD + offset + ROWS]
    psend[...] = f0 - d * lap
    f0, f1, f2 = ext[3, 0, body], ext[3, 1, body], ext[3, 2, body]
    gsend[...] = d * (3.0 * (F32(KM[3, 0]) * f0 + F32(KM[3, 1]) * f1 + F32(KM[3, 2]) * f2))
    send_g.start()
    send_p.start()

    for copy in loads[2:9]:
        copy.wait()
    basis = jnp.concatenate(
        [vin[...].astype(F32), vlev[...].astype(F32), jnp.zeros((8, 512), F32)], axis=0
    ).astype(BF16)
    read_high, read_low = split2(vread[...])
    read2 = jnp.concatenate([read_high, read_low], axis=0)
    up = nn(basis, vup[...])
    query, key, value = nn(basis, vqkv[0]), nn(basis, vqkv[1]), nn(basis, vqkv[2])
    both = nt(read2, vwout[...])
    out_read = both[:NV] + both[NV:]
    both = nt(read2, vdown[...])
    down_read = (both[:NV] + both[NV:]) * 0.5
    lane = iota((1, 128), 1)
    heads = (lane < HEAD, lane >= HEAD)
    key = key[:24] * (1.0 / math.sqrt(HEAD))
    zero_key = jnp.zeros((48, 128), F32)
    zero_out = jnp.zeros((32, 128), F32)
    keys = jnp.concatenate([jnp.where(h, key, 0.0) for h in heads], axis=0)
    outs = jnp.concatenate([jnp.where(h, out_read, 0.0) for h in heads], axis=0)
    right = jnp.concatenate(
        [
            jnp.concatenate([keys, zero_key], axis=1),
            jnp.concatenate([zero_out, outs], axis=1),
            jnp.zeros((48, 256), F32),
        ],
        axis=0,
    )
    attend = nt(jnp.concatenate([query, value], axis=1), right, HIGHEST)
    msg[0, 0:32, 0:512] = up.astype(BF16)
    msg[0, 0:32, 512:640] = attend.astype(BF16)
    msg[0, 32:48, 0:512] = down_read.astype(BF16)
    msg[0, 32:48, 512:640] = jnp.zeros((16, 128), BF16)
    msgs = []
    for r in (2, 3, 1):
        copy = pltpu.make_async_remote_copy(
            src_ref=msg.at[0], dst_ref=msg.at[r], send_sem=msg_send.at[r], recv_sem=msg_recv.at[r],
            device_id={"mp": peers[r]}, device_id_type=MESH,
        )
        copy.start()
        msgs.append(copy)
    msg_of = {2: msgs[0], 3: msgs[1], 1: msgs[2]}

    gram = nt(basis, basis)
    gram_high = gram.astype(BF16)
    gram_mid, gram_low = split2(gram - gram_high.astype(F32))
    both = nt(read2, basis)
    own_high, own_low = split2(both[:NV] + both[NV:])
    left = jnp.concatenate([gram_high, gram_mid, gram_low, own_high, own_low], axis=0)

    for tile in range(7):
        at = PAD + 8 * tile
        lap = cy[0, 8 * tile : 8 * tile + 8] * ext[:, :, at - 3 : at + 5]
        for offset in range(-2, 4):
            lap = lap + cy[offset + 3, 8 * tile : 8 * tile + 8] * ext[:, :, at + offset : at + offset + 8]
        f0, f1, f2 = ext[:, 0, at : at + 8], ext[:, 1, at : at + 8], ext[:, 2, at : at + 8]
        nothing = jnp.zeros((1, 8, F), F32)
        f3 = jnp.concatenate([f0[1:], nothing], axis=0)
        into = F32(3 * KM[3, 0]) * f0 + F32(3 * KM[3, 1]) * f1 + F32(3 * KM[3, 2]) * f2
        lap0 = (
            F32(6 * KM[0, 0]) * f0 + F32(3 * KM[0, 1]) * f1 + F32(3 * KM[0, 2]) * f2 + F32(3 * KM[0, 3]) * f3
            + jnp.concatenate([nothing, into[:3]], axis=0)
        )
        lap1 = (
            F32(1.2 * KM[1, 0]) * f0 + F32(1.2 * KM[1, 1]) * f1
            + F32(1.2 * KM[1, 2]) * f2 + F32(1.2 * KM[1, 3]) * f3
        )
        lap2 = (
            F32(1.2 * KM[2, 0]) * f0 + F32(1.2 * KM[2, 1]) * f1
            + F32(1.2 * KM[2, 2]) * f2 + F32(1.2 * KM[2, 3]) * f3
        )
        rows = 8 if tile < 6 else 1
        for a, (f, along) in enumerate(((f0, lap0), (f1, lap1), (f2, lap2))):
            fresh[:, a, 8 * tile : 8 * tile + rows] = (f - d * (lap[:, a] + along))[:, :rows]

    send_f.wait_recv()
    for a, weight in enumerate((3 * KM[0, 3], 1.2 * KM[1, 3], 1.2 * KM[2, 3])):
        fresh[3, a] = fresh[3, a] - (d * F32(weight)) * f12[...]
    send_g.wait_recv()
    fresh[0, 0] = fresh[0, 0] - grecv[0:Y]
    send_p.wait_recv()
    n12[...] = precv[...] - gsend[pl.ds(first_row, 24)]
    state_copy = pltpu.make_async_copy(fresh, new_out, out_sem.at[0])
    state_copy.start()

    taps = [fresh[:, :, pl.ds(12 * j + b, 4, stride=3), :].reshape(12, 4, F) for b in range(4)]
    begin = 4 * lax.rem(j, 2)
    taps = [
        jnp.concatenate([tap, n12[pl.ds(begin + b, 4, stride=3), :][None]], axis=0)
        for b, tap in enumerate(taps)
    ]
    across = (
        0.375 * jnp.concatenate([taps[0], taps[3]], axis=1)
        + 0.5 * jnp.concatenate([taps[1], taps[2]], axis=1)
        + 0.125 * jnp.concatenate([taps[2], taps[1]], axis=1)
    )
    cells = []
    for e in range(4):
        x0, x1, x2, x3 = (across[3 * e + a] for a in range(4))
        cells.append(0.375 * x0 + 0.5 * x1 + 0.125 * x2)
        cells.append(0.125 * x1 + 0.5 * x2 + 0.375 * x3)
    cells = jnp.concatenate(cells, axis=0).astype(BF16).astype(F32)

    turned = jnp.concatenate([cells, pltpu.roll(cells, F - NV, 1)], axis=0).T
    variables = jnp.concatenate([turned[32 * p : 32 * p + NV] for p in range(4)], axis=1)
    level = (iota((16, TOK), 1) >> 6) == iota((16, TOK), 0)
    u = jnp.concatenate([variables, jnp.where(level, 1.0, 0.0).astype(F32)], axis=0)
    first = nn(left, u.astype(BF16))
    gram_u = first[0:KU] + first[KU : 2 * KU] + first[2 * KU : 3 * KU]
    total = first[3 * KU : 3 * KU + NV] + first[3 * KU + NV :]
    squares = jnp.sum(gram_u * u, axis=0, keepdims=True)
    scaled = u * lax.rsqrt(squares * F32(1.0 / 512) + F32(1e-5))
    high, low = split2(scaled)
    scaled2 = jnp.concatenate([high, low], axis=0)
    scaled_odd = lane_turn(scaled[:24], CELLS)

    row, col = iota((16, 128), 0), iota((16, 128), 1)
    summing = jnp.where((col >> 3) == row, 1.0, 0.0).astype(BF16)
    row, col = iota((256, 16), 0), iota((256, 16), 1)
    repeat = jnp.where(((row >> 5) == (col & 7)) & (((row >> 4) & 1) == (col >> 3)), 1.0, 0.0).astype(BF16)

    for r in (0, 1, 2, 3):
        if r:
            msg_of[r].wait_recv()
        folded = msg[r, 0:32, :]
        folded2 = jnp.concatenate([folded, folded], axis=0)
        reads = msg[r, 32:48, :]
        att = tn(folded2[:, 512:640], scaled2)
        prods = []
        for h in range(2):
            for k in range(LEV):
                other = lane_turn(scaled[:24] if k % 2 == 0 else scaled_odd, CELLS * (k - k % 2))
                prod = att[24 * h : 24 * h + 24] * other
                prods.append(prod[0:8] + prod[8:16] + prod[16:24])
        prods = jnp.concatenate(prods, axis=0).astype(BF16)
        expo = jnp.exp(nn(summing, prods))
        prob = jnp.concatenate(
            [e / jnp.sum(e, axis=0, keepdims=True) for e in (expo[0:8], expo[8:16])], axis=0
        ).astype(BF16)
        spread = nn(repeat, prob)
        values = att[48:80]
        values_odd = lane_turn(values, CELLS)
        mixed = None
        for k in range(LEV):
            other = lane_turn(values if k % 2 == 0 else values_odd, CELLS * (k - k % 2))
            term = spread[32 * k : 32 * k + 32] * other
            mixed = term if mixed is None else mixed + term
        total = total + mixed[0:16] + mixed[16:32]
        for part in range(2):
            cut = slice(256 * part, 256 * part + 256)
            x = tn(folded2[:, cut], scaled2)
            inner = x * (F32(math.sqrt(2 / math.pi)) + F32(math.sqrt(2 / math.pi) * 0.044715) * (x * x))
            hidden = (x + x * jnp.tanh(inner)).astype(BF16)
            total = total + nn(reads[:, cut], hidden)

    gap = jnp.zeros((16, 128), F32)
    pieces = []
    for p in range(4):
        pieces += [total[:, 128 * p : 128 * p + 128], gap]
    turned = jnp.concatenate(pieces, axis=0).T
    result = turned[:CELLS] + pltpu.roll(turned[CELLS:], NV, 1)
    for x in range(8):
        for c in range(2):
            natural[pl.ds(8 * c + x, 4, stride=16), :] = result[8 * x + 4 * c : 8 * x + 4 * c + 4]
    loads[9].wait()
    live = jnp.where(vstretch[...] >= 0, 1.0, 0.0).astype(BF16)
    pick = jnp.where((iota((CELLS, 8), 0) & 7) == iota((CELLS, 8), 1), 1.0, 0.0).astype(BF16)
    mine = iota((CELLS, 32), 1) == (iota((CELLS, 32), 0) >> 3) + 8 * j
    live = nn(jnp.where(mine, nn(pick, live), 0.0).astype(BF16), jnp.ones((32, F), BF16))
    tbuf[0] = jnp.where(live > 0.5, natural[...], 0.0).astype(BF16)

    sends = []
    for r in (2, 3, 1):
        copy = pltpu.make_async_remote_copy(
            src_ref=tbuf.at[0], dst_ref=tbuf.at[r], send_sem=t_send.at[r], recv_sem=t_recv.at[r],
            device_id={"mp": peers[r]}, device_id_type=MESH,
        )
        copy.start()
        sends.append(copy)
    sends = {2: sends[0], 3: sends[1], 1: sends[2]}
    owner = (j, peers[1], peers[2], peers[3])
    for r in (0, 1, 2, 3):
        if r:
            sends[r].wait_recv()
        tend[pl.ds(8 * owner[r], 8)] = tbuf[r].astype(F32).reshape(8, 8, F)
    tend_copy = pltpu.make_async_copy(tend, tend_out, out_sem.at[1])
    tend_copy.start()

    for copy in (send_f, send_p, send_g, *msgs, *sends.values()):
        copy.wait_send()
    state_copy.wait()
    tend_copy.wait()


def local(elems, state_field, diffusion, stretch, w_in, lemb, w_qkv, w_out, w_up, w_down, w_read):
    state = jnp.transpose(state_field, (1, 0, 2)).reshape(4, 3, Y, F)
    vm = pltpu.VMEM
    dma = pltpu.SemaphoreType.DMA
    new, tend = pl.pallas_call(
        lambda *refs: kernel(elems, *refs),
        out_shape=(
            jax.ShapeDtypeStruct((4, 3, Y, F), F32),
            jax.ShapeDtypeStruct((32, 8, F), F32),
        ),
        in_specs=[pl.BlockSpec(memory_space=pl.ANY)] * 10,
        out_specs=[pl.BlockSpec(memory_space=pl.ANY)] * 2,
        scratch_shapes=[
            vm((4, 3, Y, F), F32),
            vm((4, 3, PAD + 64, F), F32),
            vm((7, ROWS, F), F32),
            vm((4, 3, Y, F), F32),
            vm((24, F), F32),
            vm((Y, F), F32),
            vm((ROWS, F), F32),
            vm((ROWS, F), F32),
            vm((ROWS, F), F32),
            vm((24, F), F32),
            vm((1, F), F32),
            vm((8, 32), jnp.int32),
            vm((16, 512), BF16),
            vm((8, 512), BF16),
            vm((3, 512, 128), BF16),
            vm((128, 512), BF16),
            vm((512, 512), BF16),
            vm((512, 512), BF16),
            vm((16, 512), F32),
            vm((4, 48, 640), BF16),
            vm((CELLS, F), F32),
            vm((4, CELLS, F), BF16),
            vm((32, 8, F), F32),
            dma((10,)),
            dma((2,)),
            dma((3,)),
            dma((3,)),
            dma((4,)),
            dma((4,)),
            dma((4,)),
            dma((4,)),
        ],
        compiler_params=pltpu.CompilerParams(
            collective_id=0, has_side_effects=True, vmem_limit_bytes=40 * 1024 * 1024
        ),
        name="step",
    )(
        state,
        diffusion.reshape(1, F),
        jnp.transpose(stretch),
        w_in,
        lemb,
        w_qkv,
        w_out,
        w_up,
        w_down,
        jnp.transpose(w_read),
    )
    return jnp.transpose(new.reshape(12, Y, F), (1, 0, 2)), tend


def solution(mesh):
    elems = mesh.shape["elem"]
    in_specs = (
        P(None, "elem", None),
        P(),
        P(None, "elem"),
        P(),
        P(),
        P(None, None, "mp"),
        P("mp", None),
        P(None, "mp"),
        P("mp", None),
        P(),
    )
    out_specs = (P(None, "elem", None), P(None, "elem", None))
    return jax.shard_map(
        lambda *args: local(elems, *args), mesh=mesh, in_specs=in_specs, out_specs=out_specs, check_vma=False
    )
```

time: 153 us -> 37.9 us (0.25)
  waiting for transfers between devices: 52.1 us -> 0 us
  matrix products: 41.5 us -> 0 us
  Pallas kernels: 0 us -> 27.5 us
  starting transfers between devices: 22.6 us -> 0 us
  between operations: 14.7 us -> 0.67 us
  other arithmetic: 6.5 us -> 0 us
  local copies, waits for them, and re-layouts: 15.2 us -> 9.19 us
    psum x1 -> x0, waiting for transfers between devices: 42.3 us -> none  [physics(): summed = lax.psum(partial_read, 'mp')]
    dot_general x16 -> x0, matrix products: 41.5 us -> none  [the longest x1 8.6 us: physics(): processed = jnp.dot(hidden, w_down, preferred_element_type=jnp.float32)]
    pallas_call x0 -> x1, Pallas kernels: none -> 27.5 us  [local(): pl.pallas_call(lambda *refs: kernel(elems, *refs), out_shape=(jax.ShapeDt...]
    ppermute x3 -> x0, starting transfers between devices: 22.6 us -> none  [shifted(): lax.ppermute(x, axis, [(i, (i + by) % devices) for i in range(devices)])]
    ppermute x3 -> x0, waiting for transfers between devices: 9.84 us -> none  [shifted(): lax.ppermute(x, axis, [(i, (i + by) % devices) for i in range(devices)])]
    unnamed x36 -> x22, local copies, waits for them, and re-layouts: 1.39 us -> 9.19 us
    reshape x9 -> x0, local copies, waits for them, and re-layouts: 7.36 us -> none  [the longest x1 1.42 us: physics(): keys = keys.reshape(count, levels, local_heads, head_dim)]
    convert_element_type x3 -> x0, other arithmetic: 2.58 us -> none  [the longest x1 2.53 us: physics(): (embed * lax.rsqrt(jnp.mean(embed * embed, axis=-1, keepdims=True) + 1e-0...]
  transfers between devices with their start and end apart: 4 -> 0, of which waited for: 3 -> 0; matrix products, arithmetic and copies ran while one was open for 7% -> 0% of each run, Pallas kernels for 0% -> 0%
where the time goes in v1:
time: 37.9 us; the launch traced here: 37.4 us
  Pallas kernels  27.5 us (73%)
  local copies, waits for them, and re-layouts  9.19 us (24%)
  between operations  0.67 us (2%)
    pallas_call x1, Pallas kernels, local(): pl.pallas_call(lambda *refs: kernel(elems, *refs), out_shape=(jax.ShapeDt...  27.5 us
    unnamed x22, local copies, waits for them, and re-layouts  9.19 us

profile of v1, /device:TPU:1, one launch (start us, length us, event | category | flops | bytes accessed | tf_op | source)
XLA Modules:
  0.0 37.4 jit_solution(185983603791521924)
XLA Ops:
  0.6 0.0 copy-start.8
  0.6 0.0 copy-start.9
  0.7 0.7 %copy-done.8 = s32[32,8]{0,1:T(8,128)S(1)} copy-done((s32[32,8]{0,1:T(8,128)S(1)}, s32[32,8]{0,1:T(8,128)}, u32[]{:S(2)}) %copy-start.8) | copy-done | bytes 1048
  1.3 0.0 copy-done.9
  1.3 0.0 copy-start
  1.3 1.0 %copy-done = bf16[512,512]{1,0:T(8,128)(2,1)S(1)} copy-done((bf16[512,512]{1,0:T(8,128)(2,1)S(1)}, bf16[512,512]{1,0:T(8,128)(2,1)}, u32[]{:S(2)}) %copy-start) | copy-done | bytes 524312
  2.4 0.0 copy-start.1
  2.4 1.0 %copy-done.1 = bf16[512,512]{1,0:T(8,128)(2,1)S(1)} copy-done((bf16[512,512]{1,0:T(8,128)(2,1)S(1)}, bf16[512,512]{1,0:T(8,128)(2,1)}, u32[]{:S(2)}) %copy-start.1) | copy-done | bytes 524312
  3.4 0.0 copy-start.2
  3.4 1.0 %copy-done.2 = bf16[3,512,128]{2,1,0:T(8,128)(2,1)S(1)} copy-done((bf16[3,512,128]{2,1,0:T(8,128)(2,1)S(1)}, bf16[3,512,128]{2,1,0:T(8,128)(2,1)}, u32[]{:S(2)}) %copy-start.2) | copy-done | bytes 393240
  4.4 0.0 copy-start.3
  4.4 1.0 %copy-done.3 = f32[49,12,128]{2,0,1:T(8,128)S(1)} copy-done((f32[49,12,128]{2,0,1:T(8,128)S(1)}, f32[49,12,128]{2,0,1:T(8,128)}, u32[]{:S(2)}) %copy-start.3) | copy-done | bytes 301080
  5.4 0.0 copy-start.4
  5.4 0.9 %copy-done.4 = bf16[128,512]{1,0:T(8,128)(2,1)S(1)} copy-done((bf16[128,512]{1,0:T(8,128)(2,1)S(1)}, bf16[128,512]{1,0:T(8,128)(2,1)}, u32[]{:S(2)}) %copy-start.4) | copy-done | bytes 131096
  6.3 0.0 copy-start.5
  6.3 0.8 %copy-done.5 = f32[512,16]{0,1:T(8,128)S(1)} copy-done((f32[512,16]{0,1:T(8,128)S(1)}, f32[512,16]{0,1:T(8,128)}, u32[]{:S(2)}) %copy-start.5) | copy-done | bytes 32792
  7.0 0.0 copy-start.6
  7.0 0.7 %copy-done.6 = bf16[16,512]{1,0:T(8,128)(2,1)S(1)} copy-done((bf16[16,512]{1,0:T(8,128)(2,1)S(1)}, bf16[16,512]{1,0:T(8,128)(2,1)}, u32[]{:S(2)}) %copy-start.6) | copy-done | bytes 16408
  7.8 0.0 copy-start.7
  7.8 0.7 %copy-done.7 = bf16[8,512]{1,0:T(8,128)(2,1)S(1)} copy-done((bf16[8,512]{1,0:T(8,128)(2,1)S(1)}, bf16[8,512]{1,0:T(8,128)(2,1)}, u32[]{:S(2)}) %copy-start.7) | copy-done | bytes 8216
  8.5 27.5 %step.1 = (f32[4,3,49,128]{3,2,1,0:T(8,128)S(1)}, f32[32,8,128]{2,1,0:T(8,128)S(1)}) custom-call(f32[4,3,49,128]{3,2,1,0:T(8,128)S(1)} %bitcast.9, f32[1,128]{1,0:T(1,128)S(1)} %bitcast.13, s32[8,32]{1,0:T(8,128)S(1)} %bitcast.12, bf16[16,512]{1,0:T(8,128)(2,1)S(1)} %copy-done.6, bf16[8,512]{1,0:T(8,128)(2,1)S(1)} %copy-done.7, ...), custom_call_target="tpu_custom_call" | custom-call | tf_op jit(solution)/shard_map/step/pallas_call | solution.py:350
  36.0 0.7 %copy.14 = f32[49,12,128]{2,0,1:T(8,128)} copy(f32[49,12,128]{2,0,1:T(8,128)S(1)} %bitcast.10) | data formatting | bytes 602112
  36.7 0.7 %copy.15 = f32[32,8,128]{2,1,0:T(8,128)} copy(f32[32,8,128]{2,1,0:T(8,128)S(1)} %get-tuple-element.9) | data formatting | bytes 262144
Async XLA Ops:
  0.6 0.7 %copy-start.8 = (s32[32,8]{0,1:T(8,128)S(1)}, s32[32,8]{0,1:T(8,128)}, u32[]{:S(2)}) copy-start(s32[32,8]{0,1:T(8,128)} %param.12) | copy-start | bytes 3076
  0.6 0.7 %copy-start.9 = (f32[128]{0:T(128)S(1)}, f32[128]{0:T(128)}, u32[]{:S(2)}) copy-start(f32[128]{0:T(128)} %param.11) | copy-start | bytes 1540
  1.3 1.0 %copy-start = (bf16[512,512]{1,0:T(8,128)(2,1)S(1)}, bf16[512,512]{1,0:T(8,128)(2,1)}, u32[]{:S(2)}) copy-start(bf16[512,512]{1,0:T(8,128)(2,1)} %refs_7_.1) | copy-start | bytes 1572868
  2.4 1.0 %copy-start.1 = (bf16[512,512]{1,0:T(8,128)(2,1)S(1)}, bf16[512,512]{1,0:T(8,128)(2,1)}, u32[]{:S(2)}) copy-start(bf16[512,512]{1,0:T(8,128)(2,1)} %refs_8_.1) | copy-start | bytes 1572868
  3.4 1.0 %copy-start.2 = (bf16[3,512,128]{2,1,0:T(8,128)(2,1)S(1)}, bf16[3,512,128]{2,1,0:T(8,128)(2,1)}, u32[]{:S(2)}) copy-start(bf16[3,512,128]{2,1,0:T(8,128)(2,1)} %refs_5_.1) | copy-start | bytes 1179652
  4.4 1.0 %copy-start.3 = (f32[49,12,128]{2,0,1:T(8,128)S(1)}, f32[49,12,128]{2,0,1:T(8,128)}, u32[]{:S(2)}) copy-start(f32[49,12,128]{2,0,1:T(8,128)} %param.10) | copy-start | bytes 903172
  5.4 0.9 %copy-start.4 = (bf16[128,512]{1,0:T(8,128)(2,1)S(1)}, bf16[128,512]{1,0:T(8,128)(2,1)}, u32[]{:S(2)}) copy-start(bf16[128,512]{1,0:T(8,128)(2,1)} %refs_6_.1) | copy-start | bytes 393220
  6.3 0.8 %copy-start.5 = (f32[512,16]{0,1:T(8,128)S(1)}, f32[512,16]{0,1:T(8,128)}, u32[]{:S(2)}) copy-start(f32[512,16]{0,1:T(8,128)} %param.19) | copy-start | bytes 98308
  7.0 0.7 %copy-start.6 = (bf16[16,512]{1,0:T(8,128)(2,1)S(1)}, bf16[16,512]{1,0:T(8,128)(2,1)}, u32[]{:S(2)}) copy-start(bf16[16,512]{1,0:T(8,128)(2,1)} %refs_3_.1) | copy-start | bytes 49156
  7.8 0.7 %copy-start.7 = (bf16[8,512]{1,0:T(8,128)(2,1)S(1)}, bf16[8,512]{1,0:T(8,128)(2,1)}, u32[]{:S(2)}) copy-start(bf16[8,512]{1,0:T(8,128)(2,1)} %refs_4_.1) | copy-start | bytes 24580

commit v2 on v1

--- a/solution.py
+++ b/solution.py
@@ -87,11 +87,11 @@
 
 def kernel(
     elems, state, diff, stretch, w_in, lemb, w_qkv, w_out, w_up, w_down, w_read,
-    new_out, tend_out,
-    st, ext, cy, fresh, n12, f12, gsend, grecv, psend, precv,
+    fresh, tend,
+    st, ext, cy, n12, f12, gsend, grecv, psend, precv,
     vdiff, vstretch, vin, vlev, vqkv, vwout, vup, vdown, vread,
-    msg, natural, tbuf, tend,
-    load_sem, out_sem, halo_send, halo_recv, msg_send, msg_recv, t_send, t_recv,
+    msg, natural, tbuf,
+    load_sem, halo_send, halo_recv, msg_send, msg_recv, t_send, t_recv,
 ):
     me = lax.axis_index("elem")
     j = lax.axis_index("mp")
@@ -231,8 +231,6 @@
     fresh[0, 0] = fresh[0, 0] - grecv[0:Y]
     send_p.wait_recv()
     n12[...] = precv[...] - gsend[pl.ds(first_row, 24)]
-    state_copy = pltpu.make_async_copy(fresh, new_out, out_sem.at[0])
-    state_copy.start()
 
     taps = [fresh[:, :, pl.ds(12 * j + b, 4, stride=3), :].reshape(12, 4, F) for b in range(4)]
     begin = 4 * lax.rem(j, 2)
@@ -334,17 +332,26 @@
         if r:
             sends[r].wait_recv()
         tend[pl.ds(8 * owner[r], 8)] = tbuf[r].astype(F32).reshape(8, 8, F)
-    tend_copy = pltpu.make_async_copy(tend, tend_out, out_sem.at[1])
-    tend_copy.start()
 
     for copy in (send_f, send_p, send_g, *msgs, *sends.values()):
         copy.wait_send()
-    state_copy.wait()
-    tend_copy.wait()
+
+
+def store(new, tend, new_out, tend_out, sem):
+    first = pltpu.make_async_copy(new, new_out, sem.at[0])
+    second = pltpu.make_async_copy(tend, tend_out, sem.at[1])
+    first.start()
+    second.start()
+    first.wait()
+    second.wait()
 
 
 def local(elems, state_field, diffusion, stretch, w_in, lemb, w_qkv, w_out, w_up, w_down, w_read):
     state = jnp.transpose(state_field, (1, 0, 2)).reshape(4, 3, Y, F)
+    operands = (
+        state, diffusion.reshape(1, F), jnp.transpose(stretch), w_in, lemb,
+        w_qkv, w_out, w_up, w_down, jnp.transpose(w_read),
+    )
     vm = pltpu.VMEM
     dma = pltpu.SemaphoreType.DMA
     new, tend = pl.pallas_call(
@@ -353,13 +360,12 @@
             jax.ShapeDtypeStruct((4, 3, Y, F), F32),
             jax.ShapeDtypeStruct((32, 8, F), F32),
         ),
-        in_specs=[pl.BlockSpec(memory_space=pl.ANY)] * 10,
-        out_specs=[pl.BlockSpec(memory_space=pl.ANY)] * 2,
+        in_specs=[pl.BlockSpec(memory_space=pltpu.HBM)] * 10,
+        out_specs=[pl.BlockSpec(memory_space=pltpu.VMEM)] * 2,
         scratch_shapes=[
             vm((4, 3, Y, F), F32),
             vm((4, 3, PAD + 64, F), F32),
             vm((7, ROWS, F), F32),
-            vm((4, 3, Y, F), F32),
             vm((24, F), F32),
             vm((Y, F), F32),
             vm((ROWS, F), F32),
@@ -378,9 +384,7 @@
             vm((4, 48, 640), BF16),
             vm((CELLS, F), F32),
             vm((4, CELLS, F), BF16),
-            vm((32, 8, F), F32),
             dma((10,)),
-            dma((2,)),
             dma((3,)),
             dma((3,)),
             dma((4,)),
@@ -392,18 +396,7 @@
             collective_id=0, has_side_effects=True, vmem_limit_bytes=40 * 1024 * 1024
         ),
         name="step",
-    )(
-        state,
-        diffusion.reshape(1, F),
-        jnp.transpose(stretch),
-        w_in,
-        lemb,
-        w_qkv,
-        w_out,
-        w_up,
-        w_down,
-        jnp.transpose(w_read),
-    )
+    )(*(pltpu.with_memory_space_constraint(x, pltpu.HBM) for x in operands))
     return jnp.transpose(new.reshape(12, Y, F), (1, 0, 2)), tend
 
 

time: 37.9 us -> 28.9 us (0.76); the launches traced: 37.4 us -> 28.8 us
  local copies, waits for them, and re-layouts: 9.19 us -> 1.39 us
  Pallas kernels: 27.5 us -> 26.8 us
    unnamed x22 -> x2, local copies, waits for them, and re-layouts: 9.19 us -> 1.39 us
    pallas_call x1, Pallas kernels: 27.5 us -> 26.8 us  [local(): pl.pallas_call(lambda *refs: kernel(elems, *refs), out_shape=(jax.ShapeDt...]
where the time goes in v2:
time: 28.9 us; the launch traced here: 28.8 us
  Pallas kernels  26.8 us (93%)
  local copies, waits for them, and re-layouts  1.39 us (5%)
  between operations  0.64 us (2%)
    pallas_call x1, Pallas kernels, local(): pl.pallas_call(lambda *refs: kernel(elems, *refs), out_shape=(jax.ShapeDt...  26.8 us
    unnamed x2, local copies, waits for them, and re-layouts  1.39 us

profile of v2, /device:TPU:1, one launch (start us, length us, event | category | flops | bytes accessed | tf_op | source)
XLA Modules:
  0.0 28.8 jit_solution(9341110811757531730)
XLA Ops:
  0.6 26.8 %step.1 = (f32[4,3,49,128]{3,2,1,0:T(8,128)S(1)}, f32[32,8,128]{2,1,0:T(8,128)S(1)}) custom-call(f32[4,3,49,128]{3,2,1,0:T(8,128)} %bitcast.10, f32[1,128]{1,0:T(1,128)} %bitcast.13, s32[8,32]{1,0:T(8,128)} %bitcast.12, bf16[16,512]{1,0:T(8,128)(2,1)} %refs_3_.1, bf16[8,512]{1,0:T(8,128)(2,1)} %refs_4_.1, bf16[3,512,128]{2,1,0:T(8,128)(2,1)} %refs_5_.1, ...), custom_call_target="tpu_custom_call" | custom-call | tf_op jit(solution)/shard_map/step/pallas_call | solution.py:357
  27.4 0.7 %copy.14 = f32[49,12,128]{2,0,1:T(8,128)} copy(f32[49,12,128]{2,0,1:T(8,128)S(1)} %bitcast.9) | data formatting | bytes 602112
  28.2 0.7 %copy.15 = f32[32,8,128]{2,1,0:T(8,128)} copy(f32[32,8,128]{2,1,0:T(8,128)S(1)} %get-tuple-element.9) | data formatting | bytes 262144

commit v3 on v2

--- a/solution.py
+++ b/solution.py
@@ -21,7 +21,8 @@
 ROWS = 56
 PAD = 8
 CELLS = 64
-TOK = LEV * CELLS
+HALF = 32
+TOK = LEV * HALF
 KU = 32
 
 
@@ -90,14 +91,18 @@
     fresh, tend,
     st, ext, cy, n12, f12, gsend, grecv, psend, precv,
     vdiff, vstretch, vin, vlev, vqkv, vwout, vup, vdown, vread,
-    msg, natural, tbuf,
+    msg, mask, tbuf,
     load_sem, halo_send, halo_recv, msg_send, msg_recv, t_send, t_recv,
 ):
     me = lax.axis_index("elem")
     j = lax.axis_index("mp")
-    east = lax.rem(me + 1, elems)
-    west = lax.rem(me + elems - 1, elems)
     peers = (None, j + 1 - 2 * lax.rem(j, 2), lax.rem(j + 2, 4), 3 - j)
+
+    east = {"elem": lax.rem(me + 1, elems), "mp": peers[2]}
+    west = {"elem": lax.rem(me + elems - 1, elems), "mp": peers[2]}
+    barrier = pltpu.get_barrier_semaphore()
+    for place in (east, west, {"mp": peers[2]}, {"mp": peers[3]}, {"mp": peers[1]}):
+        pl.semaphore_signal(barrier, inc=1, device_id=place, device_id_type=MESH)
 
     loads = [
         pltpu.make_async_copy(src, dst, load_sem.at[i])
@@ -111,10 +116,6 @@
     for copy in loads:
         copy.start()
 
-    barrier = pltpu.get_barrier_semaphore()
-    for place in ({"elem": east}, {"elem": west}, {"mp": peers[1]}, {"mp": peers[2]}, {"mp": peers[3]}):
-        pl.semaphore_signal(barrier, inc=1, device_id=place, device_id_type=MESH)
-
     for offset in range(-3, 4):
         cy[offset + 3] = band_along_y(offset)
     ext[:, :, 0:PAD, :] = jnp.zeros((4, 3, PAD, F), F32)
@@ -127,9 +128,10 @@
         )
 
     first_row = pl.multiple_of(8 * ((3 * j) // 2), 8)
-    send_f = far(state.at[0, 0], f12, 0, {"elem": west})
-    send_p = far(psend.at[pl.ds(first_row, 24)], precv, 1, {"elem": west})
-    send_g = far(gsend, grecv, 2, {"elem": east})
+    their_row = pl.multiple_of(8 * ((3 * peers[2]) // 2), 8)
+    send_f = far(state.at[0, 0], f12, 0, west)
+    send_p = far(psend.at[pl.ds(their_row, 24)], precv, 1, west)
+    send_g = far(gsend, grecv, 2, east)
 
     pl.semaphore_wait(barrier, 5)
     send_f.start()
@@ -182,15 +184,15 @@
     msg[0, 0:32, 512:640] = attend.astype(BF16)
     msg[0, 32:48, 0:512] = down_read.astype(BF16)
     msg[0, 32:48, 512:640] = jnp.zeros((16, 128), BF16)
-    msgs = []
-    for r in (2, 3, 1):
-        copy = pltpu.make_async_remote_copy(
-            src_ref=msg.at[0], dst_ref=msg.at[r], send_sem=msg_send.at[r], recv_sem=msg_recv.at[r],
-            device_id={"mp": peers[r]}, device_id_type=MESH,
-        )
-        copy.start()
-        msgs.append(copy)
-    msg_of = {2: msgs[0], 3: msgs[1], 1: msgs[2]}
+    msg_of = {}
+    for r, held in ((2, 0), (1, 0), (3, 2)):
+        msg_of[r] = pltpu.make_async_remote_copy(
+            src_ref=msg.at[held], dst_ref=msg.at[r], send_sem=msg_send.at[r], recv_sem=msg_recv.at[r],
+            device_id={"mp": peers[r - held]}, device_id_type=MESH,
+        )
+    msg_of[2].start()
+    msg_of[1].start()
+    forward = msg_of[3]
 
     gram = nt(basis, basis)
     gram_high = gram.astype(BF16)
@@ -198,6 +200,16 @@
     both = nt(read2, basis)
     own_high, own_low = split2(both[:NV] + both[NV:])
     left = jnp.concatenate([gram_high, gram_mid, gram_low, own_high, own_low], axis=0)
+
+    loads[9].wait()
+    live = jnp.where(vstretch[...] >= 0, 1.0, 0.0).astype(BF16)
+    cell, other = iota((CELLS, 8), 0), iota((CELLS, 8), 1)
+    place = (cell >> 3) & 3
+    place = jnp.where(cell < HALF, place + 1, jnp.where(place == 0, 0, place + 4))
+    pick = jnp.where(place == other, 1.0, 0.0).astype(BF16)
+    cell, other = iota((CELLS, 32), 0), iota((CELLS, 32), 1)
+    mine = other == 8 * j + 2 * (cell & 3) + ((cell >> 2) & 1)
+    mask[...] = nn(jnp.where(mine, nn(pick, live), 0.0).astype(BF16), jnp.ones((32, F), BF16))
 
     for tile in range(7):
         at = PAD + 8 * tile
@@ -224,6 +236,145 @@
         for a, (f, along) in enumerate(((f0, lap0), (f1, lap1), (f2, lap2))):
             fresh[:, a, 8 * tile : 8 * tile + rows] = (f - d * (lap[:, a] + along))[:, :rows]
 
+    row, col = iota((16, 128), 0), iota((16, 128), 1)
+    summing = jnp.where((col >> 3) == row, 1.0, 0.0).astype(BF16)
+    row, col = iota((256, 16), 0), iota((256, 16), 1)
+    repeat = jnp.where(((row >> 5) == (col & 7)) & (((row >> 4) & 1) == (col >> 3)), 1.0, 0.0).astype(BF16)
+
+    begin = 4 * lax.rem(j, 2)
+
+    def across(x):
+        taps = [
+            n12[pl.ds(begin + b, 4, stride=3), :]
+            if x == 12
+            else fresh[x // 3, x % 3, pl.ds(12 * j + b, 4, stride=3), :]
+            for b in range(4)
+        ]
+        return (
+            0.375 * jnp.concatenate([taps[0], taps[3]], axis=0)
+            + 0.5 * jnp.concatenate([taps[1], taps[2]], axis=0)
+            + 0.125 * jnp.concatenate([taps[2], taps[1]], axis=0)
+        )
+
+    def prepare(places):
+        nodes = {x: across(x) for x in sorted({3 * (p // 2) + p % 2 + i for p in places for i in range(3)})}
+        cells = []
+        for p in places:
+            x0, x1, x2 = (nodes[3 * (p // 2) + p % 2 + i] for i in range(3))
+            cells.append(0.375 * x0 + 0.5 * x1 + 0.125 * x2 if p % 2 == 0 else 0.125 * x0 + 0.5 * x1 + 0.375 * x2)
+        cells = jnp.concatenate(cells, axis=0).astype(BF16).astype(F32)
+
+        turned = jnp.concatenate([cells] + [pltpu.roll(cells, F - NV * q, 1) for q in (1, 2, 3)], axis=0).T
+        variables = jnp.concatenate([turned[0:NV], turned[64 : 64 + NV]], axis=1)
+        level = (iota((16, TOK), 1) >> 5) == iota((16, TOK), 0)
+        u = jnp.concatenate([variables, jnp.where(level, 1.0, 0.0).astype(F32)], axis=0)
+        first = nn(left, u.astype(BF16))
+        gram_u = first[0:KU] + first[KU : 2 * KU] + first[2 * KU : 3 * KU]
+        squares = jnp.sum(gram_u * u, axis=0, keepdims=True)
+        scaled = u * lax.rsqrt(squares * F32(1.0 / 512) + F32(1e-5))
+        high, low = split2(scaled)
+        scaled2 = jnp.concatenate([high, low], axis=0)
+        return dict(
+            places=places,
+            scaled2=scaled2,
+            tokens=scaled2.astype(F32).T.astype(BF16),
+            quarter=[lane_turn(scaled[:24], HALF * k) for k in range(4)],
+            total=first[3 * KU : 3 * KU + NV] + first[3 * KU + NV :],
+            acc=None,
+            atts={},
+            sums={},
+            spreads={},
+        )
+
+    def open_share(half, r):
+        folded = msg[r, 0:32, 512:640]
+        half["atts"][r] = tn(jnp.concatenate([folded, folded], axis=0), half["scaled2"])
+
+    def hidden_units(half, r):
+        folded = msg[r, 0:32, 0:512]
+        folded2 = jnp.concatenate([folded, folded], axis=0)
+        reads = msg[r, 32:48, 0:512]
+        for part in range(2):
+            cut = slice(256 * part, 256 * part + 256)
+            x = nn(half["tokens"], folded2[:, cut])
+            inner = x * (F32(math.sqrt(2 / math.pi)) + F32(math.sqrt(2 / math.pi) * 0.044715) * (x * x))
+            hidden = (x + x * jnp.tanh(inner)).astype(BF16)
+            term = nt(hidden, reads[:, cut])
+            half["acc"] = term if half["acc"] is None else half["acc"] + term
+
+    def scores(half, r):
+        att, quarter = half["atts"][r], half["quarter"]
+        prods = []
+        for h in range(2):
+            for k in range(LEV):
+                prod = att[24 * h : 24 * h + 24] * lane_turn(quarter[k % 4], 128 * (k // 4))
+                prods.append(prod[0:8] + prod[8:16] + prod[16:24])
+        half["sums"][r] = nn(summing, jnp.concatenate(prods, axis=0).astype(BF16))
+
+    def probabilities(half, r):
+        expo = jnp.exp(half["sums"][r])
+        prob = jnp.concatenate(
+            [e / jnp.sum(e, axis=0, keepdims=True) for e in (expo[0:8], expo[8:16])], axis=0
+        ).astype(BF16)
+        half["spreads"][r] = nn(repeat, prob)
+
+    def mix(half, r):
+        att, spread = half["atts"][r], half["spreads"][r]
+        values = [lane_turn(att[48:80], HALF * k) for k in range(4)]
+        mixed = None
+        for k in range(LEV):
+            term = spread[32 * k : 32 * k + 32] * lane_turn(values[k % 4], 128 * (k // 4))
+            mixed = term if mixed is None else mixed + term
+        half["total"] = half["total"] + mixed[0:16] + mixed[16:32]
+
+    def shares(half, several):
+        for r in several:
+            open_share(half, r)
+        stages = (hidden_units, scores, probabilities, mix)
+        for step in range(len(several) + 3):
+            for i, stage in enumerate(stages):
+                if 0 <= step - i < len(several):
+                    stage(half, several[step - i])
+
+    def finish(half, h):
+        total, acc = half["total"], half["acc"]
+        gap = jnp.zeros((48, 128), F32)
+        turned = jnp.concatenate([total[:, 0:128], gap, total[:, 128:256], gap], axis=0).T
+        wide = jnp.concatenate([acc, jnp.zeros((TOK, F - NV), F32)], axis=1)
+        turned = turned + wide[0:128] + pltpu.roll(wide[128:256], 64, 1)
+        result = turned[0:HALF]
+        for q in (1, 2, 3):
+            result = result + pltpu.roll(turned[HALF * q : HALF * q + HALF], NV * q, 1)
+        result = jnp.where(mask[HALF * h : HALF * h + HALF] > 0.5, result, 0.0)
+        tbuf[0, h] = result.astype(BF16)
+        copies = {}
+        for r in (2, 3, 1):
+            copies[r] = pltpu.make_async_remote_copy(
+                src_ref=tbuf.at[0, h], dst_ref=tbuf.at[r, h], send_sem=t_send.at[r, h], recv_sem=t_recv.at[r, h],
+                device_id={"mp": peers[r]}, device_id_type=MESH,
+            )
+            copies[r].start()
+        return copies
+
+    owner = (j, peers[1], peers[2], peers[3])
+
+    def place_rows(half, h, r):
+        block = tbuf[r, h].astype(F32)
+        for i, p in enumerate(half["places"]):
+            for c in range(2):
+                tend[pl.ds(64 * owner[r] + 8 * c + p, 4, stride=16), :] = block[8 * i + 4 * c : 8 * i + 4 * c + 4]
+
+    inner_half = prepare((1, 2, 3, 4))
+    shares(inner_half, (0,))
+    msg_of[1].wait_recv()
+    shares(inner_half, (1,))
+    msg_of[2].wait_recv()
+    forward.start()
+    shares(inner_half, (2,))
+    msg_of[3].wait_recv()
+    shares(inner_half, (3,))
+    inner_sends = finish(inner_half, 0)
+
     send_f.wait_recv()
     for a, weight in enumerate((3 * KM[0, 3], 1.2 * KM[1, 3], 1.2 * KM[2, 3])):
         fresh[3, a] = fresh[3, a] - (d * F32(weight)) * f12[...]
@@ -231,119 +382,22 @@
     fresh[0, 0] = fresh[0, 0] - grecv[0:Y]
     send_p.wait_recv()
     n12[...] = precv[...] - gsend[pl.ds(first_row, 24)]
-
-    taps = [fresh[:, :, pl.ds(12 * j + b, 4, stride=3), :].reshape(12, 4, F) for b in range(4)]
-    begin = 4 * lax.rem(j, 2)
-    taps = [
-        jnp.concatenate([tap, n12[pl.ds(begin + b, 4, stride=3), :][None]], axis=0)
-        for b, tap in enumerate(taps)
-    ]
-    across = (
-        0.375 * jnp.concatenate([taps[0], taps[3]], axis=1)
-        + 0.5 * jnp.concatenate([taps[1], taps[2]], axis=1)
-        + 0.125 * jnp.concatenate([taps[2], taps[1]], axis=1)
-    )
-    cells = []
-    for e in range(4):
-        x0, x1, x2, x3 = (across[3 * e + a] for a in range(4))
-        cells.append(0.375 * x0 + 0.5 * x1 + 0.125 * x2)
-        cells.append(0.125 * x1 + 0.5 * x2 + 0.375 * x3)
-    cells = jnp.concatenate(cells, axis=0).astype(BF16).astype(F32)
-
-    turned = jnp.concatenate([cells, pltpu.roll(cells, F - NV, 1)], axis=0).T
-    variables = jnp.concatenate([turned[32 * p : 32 * p + NV] for p in range(4)], axis=1)
-    level = (iota((16, TOK), 1) >> 6) == iota((16, TOK), 0)
-    u = jnp.concatenate([variables, jnp.where(level, 1.0, 0.0).astype(F32)], axis=0)
-    first = nn(left, u.astype(BF16))
-    gram_u = first[0:KU] + first[KU : 2 * KU] + first[2 * KU : 3 * KU]
-    total = first[3 * KU : 3 * KU + NV] + first[3 * KU + NV :]
-    squares = jnp.sum(gram_u * u, axis=0, keepdims=True)
-    scaled = u * lax.rsqrt(squares * F32(1.0 / 512) + F32(1e-5))
-    high, low = split2(scaled)
-    scaled2 = jnp.concatenate([high, low], axis=0)
-    scaled_odd = lane_turn(scaled[:24], CELLS)
-
-    row, col = iota((16, 128), 0), iota((16, 128), 1)
-    summing = jnp.where((col >> 3) == row, 1.0, 0.0).astype(BF16)
-    row, col = iota((256, 16), 0), iota((256, 16), 1)
-    repeat = jnp.where(((row >> 5) == (col & 7)) & (((row >> 4) & 1) == (col >> 3)), 1.0, 0.0).astype(BF16)
-
-    for r in (0, 1, 2, 3):
-        if r:
-            msg_of[r].wait_recv()
-        folded = msg[r, 0:32, :]
-        folded2 = jnp.concatenate([folded, folded], axis=0)
-        reads = msg[r, 32:48, :]
-        att = tn(folded2[:, 512:640], scaled2)
-        prods = []
-        for h in range(2):
-            for k in range(LEV):
-                other = lane_turn(scaled[:24] if k % 2 == 0 else scaled_odd, CELLS * (k - k % 2))
-                prod = att[24 * h : 24 * h + 24] * other
-                prods.append(prod[0:8] + prod[8:16] + prod[16:24])
-        prods = jnp.concatenate(prods, axis=0).astype(BF16)
-        expo = jnp.exp(nn(summing, prods))
-        prob = jnp.concatenate(
-            [e / jnp.sum(e, axis=0, keepdims=True) for e in (expo[0:8], expo[8:16])], axis=0
-        ).astype(BF16)
-        spread = nn(repeat, prob)
-        values = att[48:80]
-        values_odd = lane_turn(values, CELLS)
-        mixed = None
-        for k in range(LEV):
-            other = lane_turn(values if k % 2 == 0 else values_odd, CELLS * (k - k % 2))
-            term = spread[32 * k : 32 * k + 32] * other
-            mixed = term if mixed is None else mixed + term
-        total = total + mixed[0:16] + mixed[16:32]
-        for part in range(2):
-            cut = slice(256 * part, 256 * part + 256)
-            x = tn(folded2[:, cut], scaled2)
-            inner = x * (F32(math.sqrt(2 / math.pi)) + F32(math.sqrt(2 / math.pi) * 0.044715) * (x * x))
-            hidden = (x + x * jnp.tanh(inner)).astype(BF16)
-            total = total + nn(reads[:, cut], hidden)
-
-    gap = jnp.zeros((16, 128), F32)
-    pieces = []
-    for p in range(4):
-        pieces += [total[:, 128 * p : 128 * p + 128], gap]
-    turned = jnp.concatenate(pieces, axis=0).T
-    result = turned[:CELLS] + pltpu.roll(turned[CELLS:], NV, 1)
-    for x in range(8):
-        for c in range(2):
-            natural[pl.ds(8 * c + x, 4, stride=16), :] = result[8 * x + 4 * c : 8 * x + 4 * c + 4]
-    loads[9].wait()
-    live = jnp.where(vstretch[...] >= 0, 1.0, 0.0).astype(BF16)
-    pick = jnp.where((iota((CELLS, 8), 0) & 7) == iota((CELLS, 8), 1), 1.0, 0.0).astype(BF16)
-    mine = iota((CELLS, 32), 1) == (iota((CELLS, 32), 0) >> 3) + 8 * j
-    live = nn(jnp.where(mine, nn(pick, live), 0.0).astype(BF16), jnp.ones((32, F), BF16))
-    tbuf[0] = jnp.where(live > 0.5, natural[...], 0.0).astype(BF16)
-
-    sends = []
-    for r in (2, 3, 1):
-        copy = pltpu.make_async_remote_copy(
-            src_ref=tbuf.at[0], dst_ref=tbuf.at[r], send_sem=t_send.at[r], recv_sem=t_recv.at[r],
-            device_id={"mp": peers[r]}, device_id_type=MESH,
-        )
-        copy.start()
-        sends.append(copy)
-    sends = {2: sends[0], 3: sends[1], 1: sends[2]}
-    owner = (j, peers[1], peers[2], peers[3])
-    for r in (0, 1, 2, 3):
-        if r:
-            sends[r].wait_recv()
-        tend[pl.ds(8 * owner[r], 8)] = tbuf[r].astype(F32).reshape(8, 8, F)
-
-    for copy in (send_f, send_p, send_g, *msgs, *sends.values()):
+    outer_half = prepare((0, 5, 6, 7))
+    shares(outer_half, (0, 1, 2, 3))
+    outer_sends = finish(outer_half, 1)
+
+    place_rows(inner_half, 0, 0)
+    place_rows(outer_half, 1, 0)
+    for r in (1, 2, 3):
+        inner_sends[r].wait_recv()
+        place_rows(inner_half, 0, r)
+    for r in (1, 2, 3):
+        outer_sends[r].wait_recv()
+        place_rows(outer_half, 1, r)
+
+    sent = (send_f, send_p, send_g, *msg_of.values(), *inner_sends.values(), *outer_sends.values())
+    for copy in sent:
         copy.wait_send()
-
-
-def store(new, tend, new_out, tend_out, sem):
-    first = pltpu.make_async_copy(new, new_out, sem.at[0])
-    second = pltpu.make_async_copy(tend, tend_out, sem.at[1])
-    first.start()
-    second.start()
-    first.wait()
-    second.wait()
 
 
 def local(elems, state_field, diffusion, stretch, w_in, lemb, w_qkv, w_out, w_up, w_down, w_read):
@@ -358,7 +412,7 @@
         lambda *refs: kernel(elems, *refs),
         out_shape=(
             jax.ShapeDtypeStruct((4, 3, Y, F), F32),
-            jax.ShapeDtypeStruct((32, 8, F), F32),
+            jax.ShapeDtypeStruct((256, F), F32),
         ),
         in_specs=[pl.BlockSpec(memory_space=pltpu.HBM)] * 10,
         out_specs=[pl.BlockSpec(memory_space=pltpu.VMEM)] * 2,
@@ -383,21 +437,21 @@
             vm((16, 512), F32),
             vm((4, 48, 640), BF16),
             vm((CELLS, F), F32),
-            vm((4, CELLS, F), BF16),
+            vm((4, 2, HALF, F), BF16),
             dma((10,)),
             dma((3,)),
             dma((3,)),
             dma((4,)),
             dma((4,)),
-            dma((4,)),
-            dma((4,)),
+            dma((4, 2)),
+            dma((4, 2)),
         ],
         compiler_params=pltpu.CompilerParams(
             collective_id=0, has_side_effects=True, vmem_limit_bytes=40 * 1024 * 1024
         ),
         name="step",
     )(*(pltpu.with_memory_space_constraint(x, pltpu.HBM) for x in operands))
-    return jnp.transpose(new.reshape(12, Y, F), (1, 0, 2)), tend
+    return jnp.transpose(new.reshape(12, Y, F), (1, 0, 2)), tend.reshape(32, 8, F)
 
 
 def solution(mesh):

time: 28.9 us -> 28.2 us (0.976)
  Pallas kernels: 26.8 us -> 26.1 us
    pallas_call x1, Pallas kernels: 26.8 us -> 26.1 us  [local(): pl.pallas_call(lambda *refs: kernel(elems, *refs), out_shape=(jax.ShapeDt...]
where the time goes in v3:
time: 28.2 us; the launch traced here: 28.1 us
  Pallas kernels  26.1 us (93%)
  local copies, waits for them, and re-layouts  1.39 us (5%)
  between operations  0.64 us (2%)
    pallas_call x1, Pallas kernels, local(): pl.pallas_call(lambda *refs: kernel(elems, *refs), out_shape=(jax.ShapeDt...  26.1 us
    unnamed x2, local copies, waits for them, and re-layouts  1.39 us

profile of v3, /device:TPU:1, one launch (start us, length us, event | category | flops | bytes accessed | tf_op | source)
XLA Modules:
  0.0 28.1 jit_solution(10208695216908721763)
XLA Ops:
  0.6 26.1 %step.1 = (f32[4,3,49,128]{3,2,1,0:T(8,128)S(1)}, f32[256,128]{1,0:T(8,128)S(1)}) custom-call(f32[4,3,49,128]{3,2,1,0:T(8,128)} %bitcast.12, f32[1,128]{1,0:T(1,128)} %bitcast.15, s32[8,32]{1,0:T(8,128)} %bitcast.14, bf16[16,512]{1,0:T(8,128)(2,1)} %refs_3_.1, bf16[8,512]{1,0:T(8,128)(2,1)} %refs_4_.1, bf16[3,512,128]{2,1,0:T(8,128)(2,1)} %refs_5_.1, ...), custom_call_target="tpu_custom_call" | custom-call | tf_op jit(solution)/shard_map/step/pallas_call | solution.py:411
  26.7 0.7 %copy.14 = f32[49,12,128]{2,0,1:T(8,128)} copy(f32[49,12,128]{2,0,1:T(8,128)S(1)} %bitcast.10) | data formatting | bytes 602112
  27.4 0.7 %copy.15 = f32[32,8,128]{2,1,0:T(8,128)} copy(f32[32,8,128]{2,1,0:T(8,128)S(1)} %bitcast.11) | data formatting | bytes 262144

commit v4 on v3

--- a/solution.py
+++ b/solution.py
@@ -20,9 +20,8 @@
 Y = 49
 ROWS = 56
 PAD = 8
-CELLS = 64
-HALF = 32
-TOK = LEV * HALF
+ACROSS = 16
+CELLS = 8 * ACROSS
 KU = 32
 
 
@@ -89,20 +88,27 @@
 def kernel(
     elems, state, diff, stretch, w_in, lemb, w_qkv, w_out, w_up, w_down, w_read,
     fresh, tend,
-    st, ext, cy, n12, f12, gsend, grecv, psend, precv,
+    st, ext, cy, n12, gown, f12, gsend, grecv, psend, precv,
     vdiff, vstretch, vin, vlev, vqkv, vwout, vup, vdown, vread,
-    msg, mask, tbuf,
-    load_sem, halo_send, halo_recv, msg_send, msg_recv, t_send, t_recv,
+    msg, mask, tbuf0, tbuf1,
+    load_sem, halo_send, halo_recv, msg_send, msg_recv, t_send, t_recv, west_in,
 ):
     me = lax.axis_index("elem")
     j = lax.axis_index("mp")
+    tbufs = (tbuf0, tbuf1)
     peers = (None, j + 1 - 2 * lax.rem(j, 2), lax.rem(j + 2, 4), 3 - j)
 
+    core = lax.rem(j, 2)
     east = {"elem": lax.rem(me + 1, elems), "mp": peers[2]}
     west = {"elem": lax.rem(me + elems - 1, elems), "mp": peers[2]}
+
     barrier = pltpu.get_barrier_semaphore()
-    for place in (east, west, {"mp": peers[2]}, {"mp": peers[3]}, {"mp": peers[1]}):
+    for place in (west, {"mp": peers[2]}, {"mp": peers[3]}, {"mp": peers[1]}):
         pl.semaphore_signal(barrier, inc=1, device_id=place, device_id_type=MESH)
+
+    @pl.when(me != elems - 1)
+    def _():
+        pl.semaphore_signal(barrier, inc=1, device_id=east, device_id_type=MESH)
 
     loads = [
         pltpu.make_async_copy(src, dst, load_sem.at[i])
@@ -127,29 +133,25 @@
             device_id=place, device_id_type=MESH,
         )
 
-    first_row = pl.multiple_of(8 * ((3 * j) // 2), 8)
-    their_row = pl.multiple_of(8 * ((3 * peers[2]) // 2), 8)
+    first_row = pl.multiple_of(24 * core, 8)
     send_f = far(state.at[0, 0], f12, 0, west)
-    send_p = far(psend.at[pl.ds(their_row, 24)], precv, 1, west)
+    send_p = far(psend.at[pl.ds(first_row, 32)], precv, 1, west)
     send_g = far(gsend, grecv, 2, east)
-
-    pl.semaphore_wait(barrier, 5)
-    send_f.start()
 
     loads[0].wait()
     loads[1].wait()
+    d = vdiff[...]
+    share = d * (3.0 * (F32(KM[3, 0]) * st[3, 0] + F32(KM[3, 1]) * st[3, 1] + F32(KM[3, 2]) * st[3, 2]))
+    gown[0:Y] = share
+    gsend[...] = jnp.concatenate([share, jnp.zeros((64 - Y, F), F32)], axis=0).astype(BF16)
+
     ext[:, :, PAD : PAD + Y, :] = st[...]
-    d = vdiff[...]
     body = slice(PAD, PAD + ROWS)
     f0, f1, f2, f3 = ext[0, 0, body], ext[0, 1, body], ext[0, 2, body], ext[1, 0, body]
     lap = 3.0 * (F32(2 * KM[0, 0]) * f0 + F32(KM[0, 1]) * f1 + F32(KM[0, 2]) * f2 + F32(KM[0, 3]) * f3)
     for offset in range(-3, 4):
         lap = lap + cy[offset + 3] * ext[0, 0, PAD + offset : PAD + offset + ROWS]
     psend[...] = f0 - d * lap
-    f0, f1, f2 = ext[3, 0, body], ext[3, 1, body], ext[3, 2, body]
-    gsend[...] = d * (3.0 * (F32(KM[3, 0]) * f0 + F32(KM[3, 1]) * f1 + F32(KM[3, 2]) * f2))
-    send_g.start()
-    send_p.start()
 
     for copy in loads[2:9]:
         copy.wait()
@@ -180,35 +182,50 @@
         axis=0,
     )
     attend = nt(jnp.concatenate([query, value], axis=1), right, HIGHEST)
-    msg[0, 0:32, 0:512] = up.astype(BF16)
-    msg[0, 0:32, 512:640] = attend.astype(BF16)
-    msg[0, 32:48, 0:512] = down_read.astype(BF16)
-    msg[0, 32:48, 512:640] = jnp.zeros((16, 128), BF16)
-    msg_of = {}
-    for r, held in ((2, 0), (1, 0), (3, 2)):
-        msg_of[r] = pltpu.make_async_remote_copy(
-            src_ref=msg.at[held], dst_ref=msg.at[r], send_sem=msg_send.at[r], recv_sem=msg_recv.at[r],
-            device_id={"mp": peers[r - held]}, device_id_type=MESH,
-        )
-    msg_of[2].start()
-    msg_of[1].start()
-    forward = msg_of[3]
+    msg[j, 0:32, 0:512] = up.astype(BF16)
+    msg[j, 0:32, 512:640] = attend.astype(BF16)
+    msg[j, 32:48, 0:512] = down_read.astype(BF16)
+    msg[j, 32:48, 512:640] = jnp.zeros((16, 128), BF16)
+    def share_copy(owner, k, place):
+        return pltpu.make_async_remote_copy(
+            src_ref=msg.at[owner], dst_ref=msg.at[owner], send_sem=msg_send.at[k], recv_sem=msg_recv.at[k],
+            device_id={"mp": place}, device_id_type=MESH,
+        )
+
+    to_core = share_copy(j, 0, peers[1])
+    to_chip = share_copy(j, 1, peers[2])
+    onward = share_copy(peers[2], 2, peers[1])
+
+    pl.semaphore_wait(barrier, jnp.where(me == 0, 4, 5))
+    send_g.start()
+
+    @pl.when(me == elems - 1)
+    def _():
+        pl.semaphore_signal(west_in, inc=1, device_id=east, device_id_type=MESH)
+
+    @pl.when(me != 0)
+    def _():
+        send_f.start()
+        send_p.start()
+
+    to_core.start()
+    to_chip.start()
 
     gram = nt(basis, basis)
     gram_high = gram.astype(BF16)
     gram_mid, gram_low = split2(gram - gram_high.astype(F32))
     both = nt(read2, basis)
-    own_high, own_low = split2(both[:NV] + both[NV:])
+    own_high, own_low = split2((both[:NV] + both[NV:]) * 0.5)
     left = jnp.concatenate([gram_high, gram_mid, gram_low, own_high, own_low], axis=0)
 
     loads[9].wait()
     live = jnp.where(vstretch[...] >= 0, 1.0, 0.0).astype(BF16)
-    cell, other = iota((CELLS, 8), 0), iota((CELLS, 8), 1)
-    place = (cell >> 3) & 3
-    place = jnp.where(cell < HALF, place + 1, jnp.where(place == 0, 0, place + 4))
-    pick = jnp.where(place == other, 1.0, 0.0).astype(BF16)
-    cell, other = iota((CELLS, 32), 0), iota((CELLS, 32), 1)
-    mine = other == 8 * j + 2 * (cell & 3) + ((cell >> 2) & 1)
+    cell, other = iota((CELLS + 32, 8), 0), iota((CELLS + 32, 8), 1)
+    pick = jnp.where(jnp.where(cell < CELLS, cell >> 4, 0) == other, 1.0, 0.0).astype(BF16)
+    cell, other = iota((CELLS + 32, 32), 0), iota((CELLS + 32, 32), 1)
+    part_row = ACROSS * core + 2 * (cell & 7) + ((cell >> 3) & 1)
+    whole_row = 2 * (cell & 15) + ((cell >> 4) & 1)
+    mine = other == jnp.where(cell < CELLS, part_row, whole_row)
     mask[...] = nn(jnp.where(mine, nn(pick, live), 0.0).astype(BF16), jnp.ones((32, F), BF16))
 
     for tile in range(7):
@@ -241,32 +258,31 @@
     row, col = iota((256, 16), 0), iota((256, 16), 1)
     repeat = jnp.where(((row >> 5) == (col & 7)) & (((row >> 4) & 1) == (col >> 3)), 1.0, 0.0).astype(BF16)
 
-    begin = 4 * lax.rem(j, 2)
-
-    def across(x):
-        taps = [
-            n12[pl.ds(begin + b, 4, stride=3), :]
+    def across(x, whole):
+        begin, rows = (0, 16) if whole else (24 * core, 8)
+        t0, t1, t2, t3 = (
+            n12[pl.ds(b, 8, stride=3), :]
             if x == 12
-            else fresh[x // 3, x % 3, pl.ds(12 * j + b, 4, stride=3), :]
+            else fresh[x // 3, x % 3, pl.ds(begin + b, rows, stride=3), :]
             for b in range(4)
-        ]
-        return (
-            0.375 * jnp.concatenate([taps[0], taps[3]], axis=0)
-            + 0.5 * jnp.concatenate([taps[1], taps[2]], axis=0)
-            + 0.125 * jnp.concatenate([taps[2], taps[1]], axis=0)
-        )
-
-    def prepare(places):
-        nodes = {x: across(x) for x in sorted({3 * (p // 2) + p % 2 + i for p in places for i in range(3)})}
+        )
+        return jnp.concatenate([0.375 * t0 + 0.5 * t1 + 0.125 * t2, 0.125 * t1 + 0.5 * t2 + 0.375 * t3], axis=0)
+
+    def prepare(number, places, slots, whole=False):
+        nodes = {x: across(x, whole) for x in sorted({3 * (p // 2) + p % 2 + i for p in places for i in range(3)})}
         cells = []
         for p in places:
             x0, x1, x2 = (nodes[3 * (p // 2) + p % 2 + i] for i in range(3))
             cells.append(0.375 * x0 + 0.5 * x1 + 0.125 * x2 if p % 2 == 0 else 0.125 * x0 + 0.5 * x1 + 0.375 * x2)
         cells = jnp.concatenate(cells, axis=0).astype(BF16).astype(F32)
 
-        turned = jnp.concatenate([cells] + [pltpu.roll(cells, F - NV * q, 1) for q in (1, 2, 3)], axis=0).T
-        variables = jnp.concatenate([turned[0:NV], turned[64 : 64 + NV]], axis=1)
-        level = (iota((16, TOK), 1) >> 5) == iota((16, TOK), 0)
+        count = (32 if whole else ACROSS) * len(places)
+        tok, per = LEV * count, F // count
+        turned = jnp.concatenate([cells] + [pltpu.roll(cells, F - NV * q, 1) for q in range(1, per)], axis=0).T
+        variables = jnp.concatenate(
+            [turned[NV * per * t : NV * per * t + NV] for t in range(LEV // per)], axis=1
+        )
+        level = iota((16, tok), 1) // count == iota((16, tok), 0)
         u = jnp.concatenate([variables, jnp.where(level, 1.0, 0.0).astype(F32)], axis=0)
         first = nn(left, u.astype(BF16))
         gram_u = first[0:KU] + first[KU : 2 * KU] + first[2 * KU : 3 * KU]
@@ -275,10 +291,14 @@
         high, low = split2(scaled)
         scaled2 = jnp.concatenate([high, low], axis=0)
         return dict(
+            number=number,
             places=places,
+            slots=slots,
+            count=count,
+            per=per,
             scaled2=scaled2,
             tokens=scaled2.astype(F32).T.astype(BF16),
-            quarter=[lane_turn(scaled[:24], HALF * k) for k in range(4)],
+            turns=[lane_turn(scaled[:24], count * k) for k in range(per)],
             total=first[3 * KU : 3 * KU + NV] + first[3 * KU + NV :],
             acc=None,
             atts={},
@@ -287,13 +307,14 @@
         )
 
     def open_share(half, r):
-        folded = msg[r, 0:32, 512:640]
+        folded = msg[half["slots"][r], 0:32, 512:640]
         half["atts"][r] = tn(jnp.concatenate([folded, folded], axis=0), half["scaled2"])
 
     def hidden_units(half, r):
-        folded = msg[r, 0:32, 0:512]
+        slot = half["slots"][r]
+        folded = msg[slot, 0:32, 0:512]
         folded2 = jnp.concatenate([folded, folded], axis=0)
-        reads = msg[r, 32:48, 0:512]
+        reads = msg[slot, 32:48, 0:512]
         for part in range(2):
             cut = slice(256 * part, 256 * part + 256)
             x = nn(half["tokens"], folded2[:, cut])
@@ -303,11 +324,11 @@
             half["acc"] = term if half["acc"] is None else half["acc"] + term
 
     def scores(half, r):
-        att, quarter = half["atts"][r], half["quarter"]
+        att, turns, per = half["atts"][r], half["turns"], half["per"]
         prods = []
         for h in range(2):
             for k in range(LEV):
-                prod = att[24 * h : 24 * h + 24] * lane_turn(quarter[k % 4], 128 * (k // 4))
+                prod = att[24 * h : 24 * h + 24] * lane_turn(turns[k % per], F * (k // per))
                 prods.append(prod[0:8] + prod[8:16] + prod[16:24])
         half["sums"][r] = nn(summing, jnp.concatenate(prods, axis=0).astype(BF16))
 
@@ -319,83 +340,104 @@
         half["spreads"][r] = nn(repeat, prob)
 
     def mix(half, r):
-        att, spread = half["atts"][r], half["spreads"][r]
-        values = [lane_turn(att[48:80], HALF * k) for k in range(4)]
+        att, spread, per = half["atts"][r], half["spreads"][r], half["per"]
+        values = [lane_turn(att[48:80], half["count"] * k) for k in range(per)]
         mixed = None
         for k in range(LEV):
-            term = spread[32 * k : 32 * k + 32] * lane_turn(values[k % 4], 128 * (k // 4))
+            term = spread[32 * k : 32 * k + 32] * lane_turn(values[k % per], F * (k // per))
             mixed = term if mixed is None else mixed + term
         half["total"] = half["total"] + mixed[0:16] + mixed[16:32]
 
-    def shares(half, several):
-        for r in several:
+    def shares(*pairs):
+        for half, r in pairs:
             open_share(half, r)
         stages = (hidden_units, scores, probabilities, mix)
-        for step in range(len(several) + 3):
+        for step in range(len(pairs) + 3):
             for i, stage in enumerate(stages):
-                if 0 <= step - i < len(several):
-                    stage(half, several[step - i])
-
-    def finish(half, h):
-        total, acc = half["total"], half["acc"]
-        gap = jnp.zeros((48, 128), F32)
-        turned = jnp.concatenate([total[:, 0:128], gap, total[:, 128:256], gap], axis=0).T
-        wide = jnp.concatenate([acc, jnp.zeros((TOK, F - NV), F32)], axis=1)
-        turned = turned + wide[0:128] + pltpu.roll(wide[128:256], 64, 1)
-        result = turned[0:HALF]
-        for q in (1, 2, 3):
-            result = result + pltpu.roll(turned[HALF * q : HALF * q + HALF], NV * q, 1)
-        result = jnp.where(mask[HALF * h : HALF * h + HALF] > 0.5, result, 0.0)
-        tbuf[0, h] = result.astype(BF16)
-        copies = {}
+                if 0 <= step - i < len(pairs):
+                    stage(*pairs[step - i])
+
+    def turned_back(half):
+        total, acc, count, per = half["total"], half["acc"], half["count"], half["per"]
+        tiles = LEV // per
+        pieces = []
+        for t in range(tiles):
+            pieces += [total[:, F * t : F * t + F], jnp.zeros((NV * (per - 1), F), F32)]
+        turned = jnp.concatenate(pieces, axis=0).T
+        wide = jnp.concatenate([acc, jnp.zeros((LEV * count, F - NV), F32)], axis=1)
+        for t in range(tiles):
+            block = wide[F * t : F * t + F]
+            turned = turned + (block if t == 0 else pltpu.roll(block, NV * per * t, 1))
+        result = turned[0:count]
+        for q in range(1, per):
+            result = result + pltpu.roll(turned[count * q : count * q + count], NV * q, 1)
+        return result
+
+    def finish(half, skip=0):
+        live = jnp.concatenate([mask[ACROSS * p : ACROSS * p + ACROSS] for p in half["places"]], axis=0)
+        buffer, n = tbufs[half["number"]], half["number"]
+        buffer[0] = jnp.where(live > 0.5, turned_back(half), 0.0).astype(BF16)
+        rows = pl.ds(ACROSS * skip, ACROSS * (len(half["places"]) - skip))
+        half["sends"] = {}
         for r in (2, 3, 1):
-            copies[r] = pltpu.make_async_remote_copy(
-                src_ref=tbuf.at[0, h], dst_ref=tbuf.at[r, h], send_sem=t_send.at[r, h], recv_sem=t_recv.at[r, h],
+            copy = pltpu.make_async_remote_copy(
+                src_ref=buffer.at[0, rows], dst_ref=buffer.at[r, rows], send_sem=t_send.at[n, r], recv_sem=t_recv.at[n, r],
                 device_id={"mp": peers[r]}, device_id_type=MESH,
             )
-            copies[r].start()
-        return copies
-
-    owner = (j, peers[1], peers[2], peers[3])
-
-    def place_rows(half, h, r):
-        block = tbuf[r, h].astype(F32)
-        for i, p in enumerate(half["places"]):
-            for c in range(2):
-                tend[pl.ds(64 * owner[r] + 8 * c + p, 4, stride=16), :] = block[8 * i + 4 * c : 8 * i + 4 * c + 4]
-
-    inner_half = prepare((1, 2, 3, 4))
-    shares(inner_half, (0,))
-    msg_of[1].wait_recv()
-    shares(inner_half, (1,))
-    msg_of[2].wait_recv()
-    forward.start()
-    shares(inner_half, (2,))
-    msg_of[3].wait_recv()
-    shares(inner_half, (3,))
-    inner_sends = finish(inner_half, 0)
-
+            copy.start()
+            half["sends"][r] = copy
+
+    def place_rows(half, skip=()):
+        buffer = tbufs[half["number"]]
+        for r, owner in ((0, core), (1, 1 - core)):
+            if r:
+                half["sends"][1].wait_recv()
+            half["sends"][r + 2].wait_recv()
+            block = buffer[r].astype(F32) + buffer[r + 2].astype(F32)
+            for i, p in enumerate(half["places"]):
+                for c in range(2):
+                    if p not in skip:
+                        at = ACROSS * i + 8 * c
+                        tend[pl.ds(128 * owner + 8 * c + p, 8, stride=16), :] = block[at : at + 8]
+
+    chip = (j, peers[1])
+    inner = prepare(0, (1, 2, 3, 4), chip)
+    shares((inner, 0))
+    to_core.wait_recv()
+    shares((inner, 1))
+    finish(inner)
+
+    to_chip.wait_recv()
+    onward.start()
     send_f.wait_recv()
     for a, weight in enumerate((3 * KM[0, 3], 1.2 * KM[1, 3], 1.2 * KM[2, 3])):
         fresh[3, a] = fresh[3, a] - (d * F32(weight)) * f12[...]
+    send_p.wait_recv()
+    n12[...] = precv[...] - gown[pl.ds(first_row, 32)]
+    eastern = prepare(1, (4, 5, 6, 7), chip)
+    shares((eastern, 0), (eastern, 1))
+    finish(eastern, skip=1)
+    place_rows(inner)
+
+    onward.wait_recv()
+
+    @pl.when(me == 0)
+    def _():
+        pl.semaphore_wait(west_in, 1)
+        send_f.start()
+        send_p.start()
+
     send_g.wait_recv()
-    fresh[0, 0] = fresh[0, 0] - grecv[0:Y]
-    send_p.wait_recv()
-    n12[...] = precv[...] - gsend[pl.ds(first_row, 24)]
-    outer_half = prepare((0, 5, 6, 7))
-    shares(outer_half, (0, 1, 2, 3))
-    outer_sends = finish(outer_half, 1)
-
-    place_rows(inner_half, 0, 0)
-    place_rows(outer_half, 1, 0)
-    for r in (1, 2, 3):
-        inner_sends[r].wait_recv()
-        place_rows(inner_half, 0, r)
-    for r in (1, 2, 3):
-        outer_sends[r].wait_recv()
-        place_rows(outer_half, 1, r)
-
-    sent = (send_f, send_p, send_g, *msg_of.values(), *inner_sends.values(), *outer_sends.values())
+    fresh[0, 0] = fresh[0, 0] - grecv[...].astype(F32)[0:Y]
+    western = prepare(2, (0,), (0, 1, 2, 3), whole=True)
+    western["total"] = western["total"] * 2.0
+    shares((western, 0), (western, 1), (western, 2), (western, 3))
+    result = jnp.where(mask[CELLS : CELLS + 32] > 0.5, turned_back(western), 0.0)
+    for c in range(2):
+        tend[pl.ds(8 * c, 16, stride=16), :] = result[16 * c : 16 * c + 16]
+    place_rows(eastern, skip=(4,))
+
+    sent = [send_f, send_p, send_g, to_core, to_chip, onward, *inner["sends"].values(), *eastern["sends"].values()]
     for copy in sent:
         copy.wait_send()
 
@@ -420,12 +462,13 @@
             vm((4, 3, Y, F), F32),
             vm((4, 3, PAD + 64, F), F32),
             vm((7, ROWS, F), F32),
-            vm((24, F), F32),
+            vm((32, F), F32),
+            vm((ROWS, F), F32),
             vm((Y, F), F32),
+            vm((64, F), BF16),
+            vm((64, F), BF16),
             vm((ROWS, F), F32),
-            vm((ROWS, F), F32),
-            vm((ROWS, F), F32),
-            vm((24, F), F32),
+            vm((32, F), F32),
             vm((1, F), F32),
             vm((8, 32), jnp.int32),
             vm((16, 512), BF16),
@@ -436,15 +479,17 @@
             vm((512, 512), BF16),
             vm((16, 512), F32),
             vm((4, 48, 640), BF16),
-            vm((CELLS, F), F32),
-            vm((4, 2, HALF, F), BF16),
+            vm((CELLS + 32, F), F32),
+            vm((4, 4 * ACROSS, F), BF16),
+            vm((4, 4 * ACROSS, F), BF16),
             dma((10,)),
+            dma((4,)),
             dma((3,)),
             dma((3,)),
-            dma((4,)),
-            dma((4,)),
-            dma((4, 2)),
-            dma((4, 2)),
+            dma((3,)),
+            dma((2, 4)),
+            dma((2, 4)),
+            pltpu.SemaphoreType.REGULAR,
         ],
         compiler_params=pltpu.CompilerParams(
             collective_id=0, has_side_effects=True, vmem_limit_bytes=40 * 1024 * 1024

time: 28.2 us -> 22.9 us (0.81)
  Pallas kernels: 26.1 us -> 20.7 us
    pallas_call x1, Pallas kernels: 26.1 us -> 20.7 us  [local(): pl.pallas_call(lambda *refs: kernel(elems, *refs), out_shape=(jax.ShapeDt...]
where the time goes in v4:
time: 22.9 us; the launch traced here: 22.8 us
  Pallas kernels  20.7 us (90%)
  local copies, waits for them, and re-layouts  1.39 us (6%)
  between operations  0.64 us (3%)
    pallas_call x1, Pallas kernels, local(): pl.pallas_call(lambda *refs: kernel(elems, *refs), out_shape=(jax.ShapeDt...  20.7 us
    unnamed x2, local copies, waits for them, and re-layouts  1.39 us

profile of v4, /device:TPU:1, one launch (start us, length us, event | category | flops | bytes accessed | tf_op | source)
XLA Modules:
  0.0 22.8 jit_solution(3314625837958236442)
XLA Ops:
  0.6 20.7 %step.1 = (f32[4,3,49,128]{3,2,1,0:T(8,128)S(1)}, f32[256,128]{1,0:T(8,128)S(1)}) custom-call(f32[4,3,49,128]{3,2,1,0:T(8,128)} %bitcast.12, f32[1,128]{1,0:T(1,128)} %bitcast.15, s32[8,32]{1,0:T(8,128)} %bitcast.14, bf16[16,512]{1,0:T(8,128)(2,1)} %refs_3_.1, bf16[8,512]{1,0:T(8,128)(2,1)} %refs_4_.1, bf16[3,512,128]{2,1,0:T(8,128)(2,1)} %refs_5_.1, ...), custom_call_target="tpu_custom_call" | custom-call | tf_op jit(solution)/shard_map/step/pallas_call | solution.py:453
  21.4 0.7 %copy.14 = f32[49,12,128]{2,0,1:T(8,128)} copy(f32[49,12,128]{2,0,1:T(8,128)S(1)} %bitcast.10) | data formatting | bytes 602112
  22.1 0.7 %copy.15 = f32[32,8,128]{2,1,0:T(8,128)} copy(f32[32,8,128]{2,1,0:T(8,128)S(1)} %bitcast.11) | data formatting | bytes 262144

commit v5 on v4

--- a/solution.py
+++ b/solution.py
@@ -91,7 +91,7 @@
     st, ext, cy, n12, gown, f12, gsend, grecv, psend, precv,
     vdiff, vstretch, vin, vlev, vqkv, vwout, vup, vdown, vread,
     msg, mask, tbuf0, tbuf1,
-    load_sem, halo_send, halo_recv, msg_send, msg_recv, t_send, t_recv, west_in,
+    load_sem, halo_send, halo_recv, msg_send, msg_recv, t_send, t_recv, west_in, all_in,
 ):
     me = lax.axis_index("elem")
     j = lax.axis_index("mp")
@@ -100,36 +100,36 @@
 
     core = lax.rem(j, 2)
     east = {"elem": lax.rem(me + 1, elems), "mp": peers[2]}
+    east_other = {"elem": lax.rem(me + 1, elems), "mp": peers[3]}
     west = {"elem": lax.rem(me + elems - 1, elems), "mp": peers[2]}
-
-    barrier = pltpu.get_barrier_semaphore()
-    for place in (west, {"mp": peers[2]}, {"mp": peers[3]}, {"mp": peers[1]}):
-        pl.semaphore_signal(barrier, inc=1, device_id=place, device_id_type=MESH)
-
-    @pl.when(me != elems - 1)
-    def _():
-        pl.semaphore_signal(barrier, inc=1, device_id=east, device_id_type=MESH)
+    west_first = {"elem": lax.rem(me + elems - 1, elems), "mp": peers[2] - core}
+    east_second = {"elem": lax.rem(me + 1, elems), "mp": peers[2] - core + 1}
 
     loads = [
         pltpu.make_async_copy(src, dst, load_sem.at[i])
         for i, (src, dst) in enumerate(
             [
-                (state, st), (diff, vdiff), (w_in, vin), (lemb, vlev), (w_read, vread),
+                (state.at[3], st.at[3]), (diff, vdiff), (state.at[0:3], st.at[0:3]), (w_in, vin), (lemb, vlev), (w_read, vread),
                 (w_qkv, vqkv), (w_up, vup), (w_out, vwout), (w_down, vdown), (stretch, vstretch),
             ]
         )
     ]
-    for copy in loads:
-        copy.start()
-
-    for offset in range(-3, 4):
-        cy[offset + 3] = band_along_y(offset)
-    ext[:, :, 0:PAD, :] = jnp.zeros((4, 3, PAD, F), F32)
-    ext[:, :, PAD + 48 : PAD + 64, :] = jnp.zeros((4, 3, 16, F), F32)
-
-    def far(src, dst, k, place):
+    loads[0].start()
+    loads[1].start()
+
+    barrier = pltpu.get_barrier_semaphore()
+    pl.semaphore_signal(barrier, inc=1, device_id=west_first, device_id_type=MESH)
+    pl.semaphore_signal(barrier, inc=1, device_id={"mp": peers[2] - core + 1}, device_id_type=MESH)
+
+    pl.semaphore_signal(barrier, inc=1, device_id={"mp": peers[1]}, device_id_type=MESH)
+
+    @pl.when(me != elems - 1)
+    def _():
+        pl.semaphore_signal(barrier, inc=1, device_id=east_second, device_id_type=MESH)
+
+    def far(src, dst, k, place, s=None):
         return pltpu.make_async_remote_copy(
-            src_ref=src, dst_ref=dst, send_sem=halo_send.at[k], recv_sem=halo_recv.at[k],
+            src_ref=src, dst_ref=dst, send_sem=halo_send.at[k if s is None else s], recv_sem=halo_recv.at[k],
             device_id=place, device_id_type=MESH,
         )
 
@@ -137,7 +137,10 @@
     send_f = far(state.at[0, 0], f12, 0, west)
     send_p = far(psend.at[pl.ds(first_row, 32)], precv, 1, west)
     send_g = far(gsend, grecv, 2, east)
-
+    send_g_other = far(gsend, grecv, 2, east_other, 3)
+
+    for copy in loads[2:]:
+        copy.start()
     loads[0].wait()
     loads[1].wait()
     d = vdiff[...]
@@ -145,6 +148,24 @@
     gown[0:Y] = share
     gsend[...] = jnp.concatenate([share, jnp.zeros((64 - Y, F), F32)], axis=0).astype(BF16)
 
+    @pl.when(core == 0)
+    def _():
+        pl.semaphore_wait(barrier, 3)
+
+        @pl.when(me == elems - 1)
+        def _():
+            pl.semaphore_signal(west_in, inc=1, device_id=east, device_id_type=MESH)
+            pl.semaphore_signal(west_in, inc=1, device_id=east_other, device_id_type=MESH)
+
+        send_g.start()
+        send_g_other.start()
+
+    for offset in range(-3, 4):
+        cy[offset + 3] = band_along_y(offset)
+    ext[:, :, 0:PAD, :] = jnp.zeros((4, 3, PAD, F), F32)
+    ext[:, :, PAD + 48 : PAD + 64, :] = jnp.zeros((4, 3, 16, F), F32)
+
+    loads[2].wait()
     ext[:, :, PAD : PAD + Y, :] = st[...]
     body = slice(PAD, PAD + ROWS)
     f0, f1, f2, f3 = ext[0, 0, body], ext[0, 1, body], ext[0, 2, body], ext[1, 0, body]
@@ -153,7 +174,7 @@
         lap = lap + cy[offset + 3] * ext[0, 0, PAD + offset : PAD + offset + ROWS]
     psend[...] = f0 - d * lap
 
-    for copy in loads[2:9]:
+    for copy in loads[3:10]:
         copy.wait()
     basis = jnp.concatenate(
         [vin[...].astype(F32), vlev[...].astype(F32), jnp.zeros((8, 512), F32)], axis=0
@@ -196,12 +217,15 @@
     to_chip = share_copy(j, 1, peers[2])
     onward = share_copy(peers[2], 2, peers[1])
 
-    pl.semaphore_wait(barrier, jnp.where(me == 0, 4, 5))
-    send_g.start()
-
-    @pl.when(me == elems - 1)
-    def _():
-        pl.semaphore_signal(west_in, inc=1, device_id=east, device_id_type=MESH)
+    @pl.when(core == 1)
+    def _():
+        pl.semaphore_wait(barrier, jnp.where(me == 0, 3, 5))
+        pl.semaphore_signal(all_in, inc=1, device_id={"mp": peers[1]}, device_id_type=MESH)
+
+    @pl.when(core == 0)
+    def _():
+        pl.semaphore_wait(all_in, 1)
+
 
     @pl.when(me != 0)
     def _():
@@ -218,7 +242,7 @@
     own_high, own_low = split2((both[:NV] + both[NV:]) * 0.5)
     left = jnp.concatenate([gram_high, gram_mid, gram_low, own_high, own_low], axis=0)
 
-    loads[9].wait()
+    loads[10].wait()
     live = jnp.where(vstretch[...] >= 0, 1.0, 0.0).astype(BF16)
     cell, other = iota((CELLS + 32, 8), 0), iota((CELLS + 32, 8), 1)
     pick = jnp.where(jnp.where(cell < CELLS, cell >> 4, 0) == other, 1.0, 0.0).astype(BF16)
@@ -268,8 +292,8 @@
         )
         return jnp.concatenate([0.375 * t0 + 0.5 * t1 + 0.125 * t2, 0.125 * t1 + 0.5 * t2 + 0.375 * t3], axis=0)
 
-    def prepare(number, places, slots, whole=False):
-        nodes = {x: across(x, whole) for x in sorted({3 * (p // 2) + p % 2 + i for p in places for i in range(3)})}
+    def prepare(number, places, slots, whole=False, known={}):
+        nodes = {x: known[x] if x in known else across(x, whole) for x in sorted({3 * (p // 2) + p % 2 + i for p in places for i in range(3)})}
         cells = []
         for p in places:
             x0, x1, x2 = (nodes[3 * (p // 2) + p % 2 + i] for i in range(3))
@@ -349,13 +373,14 @@
         half["total"] = half["total"] + mixed[0:16] + mixed[16:32]
 
     def shares(*pairs):
-        for half, r in pairs:
-            open_share(half, r)
-        stages = (hidden_units, scores, probabilities, mix)
-        for step in range(len(pairs) + 3):
-            for i, stage in enumerate(stages):
-                if 0 <= step - i < len(pairs):
-                    stage(*pairs[step - i])
+        for pair in pairs:
+            open_share(*pair)
+        stages = (scores, probabilities, mix)
+        for i, pair in enumerate(pairs):
+            hidden_units(*pair)
+            for stage in stages[i : i + 1] if i < len(pairs) - 1 else stages[i:]:
+                for other in pairs:
+                    stage(*other)
 
     def turned_back(half):
         total, acc, count, per = half["total"], half["acc"], half["count"], half["per"]
@@ -419,6 +444,10 @@
     finish(eastern, skip=1)
     place_rows(inner)
 
+    @pl.when(me == 0)
+    def _():
+        place_rows(eastern, skip=(4,))
+
     onward.wait_recv()
 
     @pl.when(me == 0)
@@ -427,19 +456,37 @@
         send_f.start()
         send_p.start()
 
+    known = {x: across(x, True) for x in (1, 2)}
     send_g.wait_recv()
     fresh[0, 0] = fresh[0, 0] - grecv[...].astype(F32)[0:Y]
-    western = prepare(2, (0,), (0, 1, 2, 3), whole=True)
+    western = prepare(2, (0,), (0, 1, 2, 3), whole=True, known=known)
     western["total"] = western["total"] * 2.0
     shares((western, 0), (western, 1), (western, 2), (western, 3))
     result = jnp.where(mask[CELLS : CELLS + 32] > 0.5, turned_back(western), 0.0)
     for c in range(2):
         tend[pl.ds(8 * c, 16, stride=16), :] = result[16 * c : 16 * c + 16]
-    place_rows(eastern, skip=(4,))
-
-    sent = [send_f, send_p, send_g, to_core, to_chip, onward, *inner["sends"].values(), *eastern["sends"].values()]
+
+    @pl.when(me != 0)
+    def _():
+        place_rows(eastern, skip=(4,))
+
+    sent = [send_f, send_p, to_core, to_chip, onward, *inner["sends"].values(), *eastern["sends"].values()]
     for copy in sent:
         copy.wait_send()
+
+    @pl.when(core == 0)
+    def _():
+        send_g.wait_send()
+        send_g_other.wait_send()
+
+
+def store(new, tend, new_out, tend_out, sem):
+    first = pltpu.make_async_copy(new, new_out, sem.at[0])
+    second = pltpu.make_async_copy(tend, tend_out, sem.at[1])
+    first.start()
+    second.start()
+    first.wait()
+    second.wait()
 
 
 def local(elems, state_field, diffusion, stretch, w_in, lemb, w_qkv, w_out, w_up, w_down, w_read):
@@ -482,7 +529,7 @@
             vm((CELLS + 32, F), F32),
             vm((4, 4 * ACROSS, F), BF16),
             vm((4, 4 * ACROSS, F), BF16),
-            dma((10,)),
+            dma((11,)),
             dma((4,)),
             dma((3,)),
             dma((3,)),
@@ -490,12 +537,22 @@
             dma((2, 4)),
             dma((2, 4)),
             pltpu.SemaphoreType.REGULAR,
+            pltpu.SemaphoreType.REGULAR,
         ],
         compiler_params=pltpu.CompilerParams(
             collective_id=0, has_side_effects=True, vmem_limit_bytes=40 * 1024 * 1024
         ),
         name="step",
     )(*(pltpu.with_memory_space_constraint(x, pltpu.HBM) for x in operands))
+    new, tend = (pltpu.with_memory_space_constraint(x, pltpu.VMEM) for x in (new, tend))
+    new, tend = pl.pallas_call(
+        store,
+        out_shape=(jax.ShapeDtypeStruct(new.shape, F32), jax.ShapeDtypeStruct(tend.shape, F32)),
+        in_specs=[pl.BlockSpec(memory_space=pltpu.VMEM)] * 2,
+        out_specs=[pl.BlockSpec(memory_space=pltpu.HBM)] * 2,
+        scratch_shapes=[dma((2,))],
+        name="store",
+    )(new, tend)
     return jnp.transpose(new.reshape(12, Y, F), (1, 0, 2)), tend.reshape(32, 8, F)
 
 

time: 22.9 us -> 22.2 us (0.969)
  local copies, waits for them, and re-layouts: 1.39 us -> 0 us
  Pallas kernels: 20.7 us -> 21.4 us
    unnamed x2 -> x0, local copies, waits for them, and re-layouts: 1.39 us -> none
    pallas_call x0 -> x1, Pallas kernels: none -> 0.77 us  [local(): pl.pallas_call(store, out_shape=(jax.ShapeDtypeStruct(new.shape, F32), ja...]
where the time goes in v5:
time: 22.2 us; the launch traced here: 22 us
  Pallas kernels  21.4 us (96%)
  between operations  0.64 us (3%)
    pallas_call x1, Pallas kernels, local(): pl.pallas_call(lambda *refs: kernel(elems, *refs), out_shape=(jax.ShapeDt...  20.6 us
    pallas_call x1, Pallas kernels, local(): pl.pallas_call(store, out_shape=(jax.ShapeDtypeStruct(new.shape, F32), ja...  0.77 us

profile of v5, /device:TPU:1, one launch (start us, length us, event | category | flops | bytes accessed | tf_op | source)
XLA Modules:
  0.0 22.0 jit_solution(9894671647009052720)
XLA Ops:
  0.6 20.6 %step.1 = (f32[4,3,49,128]{3,2,1,0:T(8,128)S(1)}, f32[256,128]{1,0:T(8,128)S(1)}) custom-call(f32[4,3,49,128]{3,2,1,0:T(8,128)} %bitcast.10, f32[1,128]{1,0:T(1,128)} %bitcast.13, s32[8,32]{1,0:T(8,128)} %bitcast.12, bf16[16,512]{1,0:T(8,128)(2,1)} %refs_3_.1, bf16[8,512]{1,0:T(8,128)(2,1)} %refs_4_.1, bf16[3,512,128]{2,1,0:T(8,128)(2,1)} %refs_5_.1, ...), custom_call_target="tpu_custom_call" | custom-call | tf_op jit(solution)/shard_map/step/pallas_call | solution.py:500
  21.2 0.8 %store.1 = (f32[4,3,49,128]{3,2,1,0:T(8,128)}, f32[256,128]{1,0:T(8,128)}) custom-call(f32[4,3,49,128]{3,2,1,0:T(8,128)S(1)} %get-tuple-element.6.new, f32[256,128]{1,0:T(8,128)S(1)} %get-tuple-element.7.tend), custom_call_target="tpu_custom_call" | custom-call | tf_op jit(solution)/shard_map/store/pallas_call | solution.py:548

commit v6 on v5

--- a/solution.py
+++ b/solution.py
@@ -141,6 +141,16 @@
 
     for copy in loads[2:]:
         copy.start()
+
+    @pl.when(core == 0)
+    def _():
+        pl.semaphore_wait(barrier, 3)
+
+        @pl.when(me == elems - 1)
+        def _():
+            pl.semaphore_signal(west_in, inc=1, device_id=east_other, device_id_type=MESH)
+            pl.semaphore_signal(west_in, inc=1, device_id=east, device_id_type=MESH)
+
     loads[0].wait()
     loads[1].wait()
     d = vdiff[...]
@@ -150,15 +160,8 @@
 
     @pl.when(core == 0)
     def _():
-        pl.semaphore_wait(barrier, 3)
-
-        @pl.when(me == elems - 1)
-        def _():
-            pl.semaphore_signal(west_in, inc=1, device_id=east, device_id_type=MESH)
-            pl.semaphore_signal(west_in, inc=1, device_id=east_other, device_id_type=MESH)
-
+        send_g_other.start()
         send_g.start()
-        send_g_other.start()
 
     for offset in range(-3, 4):
         cy[offset + 3] = band_along_y(offset)

time: 22.2 us -> 21.8 us (0.982)
  Pallas kernels: 21.4 us -> 21 us
    pallas_call x1, Pallas kernels: 20.6 us -> 20.3 us  [local(): pl.pallas_call(lambda *refs: kernel(elems, *refs), out_shape=(jax.ShapeDt...]
where the time goes in v6:
time: 21.8 us; the launch traced here: 21.7 us
  Pallas kernels  21 us (96%)
  between operations  0.64 us (3%)
    pallas_call x1, Pallas kernels, local(): pl.pallas_call(lambda *refs: kernel(elems, *refs), out_shape=(jax.ShapeDt...  20.3 us
    pallas_call x1, Pallas kernels, local(): pl.pallas_call(store, out_shape=(jax.ShapeDtypeStruct(new.shape, F32), ja...  0.77 us

profile of v6, /device:TPU:1, one launch (start us, length us, event | category | flops | bytes accessed | tf_op | source)
XLA Modules:
  0.0 21.7 jit_solution(5495022145227253268)
XLA Ops:
  0.6 20.3 %step.1 = (f32[4,3,49,128]{3,2,1,0:T(8,128)S(1)}, f32[256,128]{1,0:T(8,128)S(1)}) custom-call(f32[4,3,49,128]{3,2,1,0:T(8,128)} %bitcast.10, f32[1,128]{1,0:T(1,128)} %bitcast.13, s32[8,32]{1,0:T(8,128)} %bitcast.12, bf16[16,512]{1,0:T(8,128)(2,1)} %refs_3_.1, bf16[8,512]{1,0:T(8,128)(2,1)} %refs_4_.1, bf16[3,512,128]{2,1,0:T(8,128)(2,1)} %refs_5_.1, ...), custom_call_target="tpu_custom_call" | custom-call | tf_op jit(solution)/shard_map/step/pallas_call | solution.py:503
  20.9 0.8 %store.1 = (f32[4,3,49,128]{3,2,1,0:T(8,128)}, f32[256,128]{1,0:T(8,128)}) custom-call(f32[4,3,49,128]{3,2,1,0:T(8,128)S(1)} %get-tuple-element.6.new, f32[256,128]{1,0:T(8,128)S(1)} %get-tuple-element.7.tend), custom_call_target="tpu_custom_call" | custom-call | tf_op jit(solution)/shard_map/store/pallas_call | solution.py:551

commit v7 on v6

--- a/solution.py
+++ b/solution.py
@@ -313,7 +313,7 @@
         u = jnp.concatenate([variables, jnp.where(level, 1.0, 0.0).astype(F32)], axis=0)
         first = nn(left, u.astype(BF16))
         gram_u = first[0:KU] + first[KU : 2 * KU] + first[2 * KU : 3 * KU]
-        squares = jnp.sum(gram_u * u, axis=0, keepdims=True)
+        squares = jnp.maximum(jnp.sum(gram_u * u, axis=0, keepdims=True), 0.0)
         scaled = u * lax.rsqrt(squares * F32(1.0 / 512) + F32(1e-5))
         high, low = split2(scaled)
         scaled2 = jnp.concatenate([high, low], axis=0)
@@ -459,6 +459,14 @@
         send_f.start()
         send_p.start()
 
+    for copy in (to_core, to_chip, onward, *inner["sends"].values()):
+        copy.wait_send()
+
+    @pl.when(core == 0)
+    def _():
+        send_g.wait_send()
+        send_g_other.wait_send()
+
     known = {x: across(x, True) for x in (1, 2)}
     send_g.wait_recv()
     fresh[0, 0] = fresh[0, 0] - grecv[...].astype(F32)[0:Y]
@@ -473,14 +481,8 @@
     def _():
         place_rows(eastern, skip=(4,))
 
-    sent = [send_f, send_p, to_core, to_chip, onward, *inner["sends"].values(), *eastern["sends"].values()]
-    for copy in sent:
+    for copy in (send_f, send_p, *eastern["sends"].values()):
         copy.wait_send()
-
-    @pl.when(core == 0)
-    def _():
-        send_g.wait_send()
-        send_g_other.wait_send()
 
 
 def store(new, tend, new_out, tend_out, sem):

time: 21.8 us -> 21.8 us (level)
  no operation moved by 1% of the time
where the time goes in v7:
time: 21.8 us; the launch traced here: 21.7 us
  Pallas kernels  21 us (96%)
  between operations  0.64 us (3%)
    pallas_call x1, Pallas kernels, local(): pl.pallas_call(lambda *refs: kernel(elems, *refs), out_shape=(jax.ShapeDt...  20.3 us
    pallas_call x1, Pallas kernels, local(): pl.pallas_call(store, out_shape=(jax.ShapeDtypeStruct(new.shape, F32), ja...  0.77 us

profile of v7, /device:TPU:1, one launch (start us, length us, event | category | flops | bytes accessed | tf_op | source)
XLA Modules:
  0.0 21.7 jit_solution(17088949719490290634)
XLA Ops:
  0.6 20.3 %step.1 = (f32[4,3,49,128]{3,2,1,0:T(8,128)S(1)}, f32[256,128]{1,0:T(8,128)S(1)}) custom-call(f32[4,3,49,128]{3,2,1,0:T(8,128)} %bitcast.10, f32[1,128]{1,0:T(1,128)} %bitcast.13, s32[8,32]{1,0:T(8,128)} %bitcast.12, bf16[16,512]{1,0:T(8,128)(2,1)} %refs_3_.1, bf16[8,512]{1,0:T(8,128)(2,1)} %refs_4_.1, bf16[3,512,128]{2,1,0:T(8,128)(2,1)} %refs_5_.1, ...), custom_call_target="tpu_custom_call" | custom-call | tf_op jit(solution)/shard_map/step/pallas_call | solution.py:505
  20.9 0.8 %store.1 = (f32[4,3,49,128]{3,2,1,0:T(8,128)}, f32[256,128]{1,0:T(8,128)}) custom-call(f32[4,3,49,128]{3,2,1,0:T(8,128)S(1)} %get-tuple-element.6.new, f32[256,128]{1,0:T(8,128)S(1)} %get-tuple-element.7.tend), custom_call_target="tpu_custom_call" | custom-call | tf_op jit(solution)/shard_map/store/pallas_call | solution.py:553

commit v8 on v7

--- a/solution.py
+++ b/solution.py
@@ -321,6 +321,7 @@
             number=number,
             places=places,
             slots=slots,
+            whole=whole,
             count=count,
             per=per,
             scaled2=scaled2,
@@ -345,7 +346,10 @@
         for part in range(2):
             cut = slice(256 * part, 256 * part + 256)
             x = nn(half["tokens"], folded2[:, cut])
-            inner = x * (F32(math.sqrt(2 / math.pi)) + F32(math.sqrt(2 / math.pi) * 0.044715) * (x * x))
+            kind = F32
+            if half["whole"]:
+                kind, x = BF16, x.astype(BF16)
+            inner = x * (kind(math.sqrt(2 / math.pi)) + kind(math.sqrt(2 / math.pi) * 0.044715) * (x * x))
             hidden = (x + x * jnp.tanh(inner)).astype(BF16)
             term = nt(hidden, reads[:, cut])
             half["acc"] = term if half["acc"] is None else half["acc"] + term

time: 21.8 us -> 21.8 us (level)
  no operation moved by 1% of the time
where the time goes in v8:
time: 21.8 us; the launch traced here: 21.6 us
  Pallas kernels  21 us (96%)
  between operations  0.64 us (3%)
    pallas_call x1, Pallas kernels, local(): pl.pallas_call(lambda *refs: kernel(elems, *refs), out_shape=(jax.ShapeDt...  20.2 us
    pallas_call x1, Pallas kernels, local(): pl.pallas_call(store, out_shape=(jax.ShapeDtypeStruct(new.shape, F32), ja...  0.77 us

profile of v8, /device:TPU:1, one launch (start us, length us, event | category | flops | bytes accessed | tf_op | source)
XLA Modules:
  0.0 21.6 jit_solution(7875171023509937964)
XLA Ops:
  0.6 20.2 %step.1 = (f32[4,3,49,128]{3,2,1,0:T(8,128)S(1)}, f32[256,128]{1,0:T(8,128)S(1)}) custom-call(f32[4,3,49,128]{3,2,1,0:T(8,128)} %bitcast.10, f32[1,128]{1,0:T(1,128)} %bitcast.13, s32[8,32]{1,0:T(8,128)} %bitcast.12, bf16[16,512]{1,0:T(8,128)(2,1)} %refs_3_.1, bf16[8,512]{1,0:T(8,128)(2,1)} %refs_4_.1, bf16[3,512,128]{2,1,0:T(8,128)(2,1)} %refs_5_.1, ...), custom_call_target="tpu_custom_call" | custom-call | tf_op jit(solution)/shard_map/step/pallas_call | solution.py:509
  20.9 0.8 %store.1 = (f32[4,3,49,128]{3,2,1,0:T(8,128)}, f32[256,128]{1,0:T(8,128)}) custom-call(f32[4,3,49,128]{3,2,1,0:T(8,128)S(1)} %get-tuple-element.6.new, f32[256,128]{1,0:T(8,128)S(1)} %get-tuple-element.7.tend), custom_call_target="tpu_custom_call" | custom-call | tf_op jit(solution)/shard_map/store/pallas_call | solution.py:557
